TPU v7x, 32 devices: a whole 2x2x4 slice. The times are simulated.
32 devices in a mesh: section: 2 (over x), rep: 16 (over z, y, core).
Axes of the slice: x: 2, y: 2, z: 4, core: 2. Of those that a mesh axis runs over, the one named last changes fastest.
Arguments:
- ends_in: bfloat16 [2, 8192, 768], P('section', 'rep'), may hold values from -6 to 6
- lengths: int32 [16, 2, 4], P('rep'), may hold values from 0 to 256, as said below
- times: int32 [16, 2, 4], P('rep'), may hold values from 0 to 999
- norm_gain: bfloat16 [2, 768], P('section'), may hold values from 0.099609375 to 1.8984375
- attend_in: bfloat16 [2, 768, 2304], P('section'), may hold values from -0.21875 to 0.21875
- attend_out: bfloat16 [2, 768, 768], P('section'), may hold values from -1.25 to 1.25
- time_weight: bfloat16 [2, 128, 2304], P('section'), may hold values from -0.5 to 0.5
- time_bias: bfloat16 [2, 2304], P('section'), may hold values from -3 to 3
- expand_weight: bfloat16 [2, 768, 3072], P('section'), may hold values from -0.21875 to 0.21875
- expand_bias: bfloat16 [2, 3072], P('section'), may hold values from -3 to 3
- reduce_weight: bfloat16 [2, 3072, 768], P('section'), may hold values from -0.109375 to 0.109375
- reduce_bias: bfloat16 [2, 768], P('section'), may hold values from -3 to 3
Outputs:
- ends_out: bfloat16 [2, 8192, 768], P('section', 'rep')
- grad_norm_gain: float32 [2, 768], P('section', 'rep')
- grad_attend_in: float32 [2, 768, 2304], P('section', 'rep')
- grad_attend_out: float32 [2, 768, 768], P('section', 'rep')
- grad_time_weight: float32 [2, 128, 2304], P('section', 'rep')
- grad_time_bias: float32 [2, 2304], P('section', 'rep')
- grad_expand_weight: float32 [2, 768, 3072], P('section', 'rep')
- grad_expand_bias: float32 [2, 3072], P('section', 'rep')
- grad_reduce_weight: float32 [2, 3072, 768], P('section', 'rep')
- grad_reduce_bias: float32 [2, 768], P('section', 'rep')
Inputs may be any that keep to these rules, and one draw needn't show every extreme that they name: Each micro-batch's 4 lengths sum to 256: either one sequence of 256 tokens followed by zeros, or 4 sequences of 64 tokens; some micro-batch of some replica holds one sequence.
All inputs are finite; a program needn't handle non-finite values.
Results may differ from a plain program's by a relative error of at most 0.019.
Values may be sent and summed in bfloat16 or wider, within the bound.
No kernel may reach another device: no remote copies, remote signals or barrier semaphores. Data moves between devices by JAX's collectives and lax.ppermute only.
A program may use at most 192 MiB of HBM per device.

v0:
```python
from functools import partial
import math

import jax
import jax.numpy as jnp
from jax import lax
from jax.sharding import PartitionSpec as P

HEADS = 12
HEAD = 64
EMB = 128
SEGS = 4


def from_behind(block, axis, distance):
    devices = range(lax.axis_size(axis))
    route = [(i - distance, i) for i in devices if i - distance in devices]
    return lax.ppermute(block, axis, route)


def normalize(values):
    center = values - jnp.mean(values, axis=-1, keepdims=True)
    spread = jnp.mean(center * center, axis=-1, keepdims=True)
    return center * lax.rsqrt(spread + 1e-05)


def segment_table(lengths_row, times_row, span):
    finish = jnp.cumsum(lengths_row)
    begin = finish - lengths_row
    position = jnp.arange(span, dtype=jnp.int32)
    owner = jnp.sum((position[:, None] >= finish[None, :]).astype(jnp.int32), axis=1)
    member = owner[:, None] == jnp.arange(SEGS, dtype=jnp.int32)[None, :]
    onehot = member.astype(jnp.float32)
    offset = jnp.sum(jnp.where(member, begin[None, :], 0), axis=1)
    place = (position - offset).astype(jnp.float32)
    same = owner[:, None] == owner[None, :]
    freqs = jnp.exp(-math.log(10000.0) * jnp.arange(EMB // 2, dtype=jnp.float32) / (EMB // 2))
    phase = times_row.astype(jnp.float32)[:, None] * freqs[None, :]
    embed = jnp.concatenate([jnp.cos(phase), jnp.sin(phase)], axis=1)
    return (onehot, place, same, embed)


def angles(place):
    half_size = HEAD // 2
    freqs = jnp.exp(-math.log(10000.0) * jnp.arange(half_size, dtype=jnp.float32) / half_size)
    phase = place[:, None, None] * freqs[None, None, :]
    return (jnp.cos(phase), jnp.sin(phase))


def rotate(values, cos_part, sin_part):
    half_size = values.shape[-1] // 2
    first_half = values[..., :half_size]
    second_half = values[..., half_size:]
    return jnp.concatenate(
        [
            first_half * cos_part - second_half * sin_part,
            second_half * cos_part + first_half * sin_part,
        ],
        axis=-1,
    )


def modulation(time_weight, time_bias, onehot, embed, width):
    per_seq = jnp.dot(
        embed, time_weight.astype(jnp.float32), precision=lax.Precision.HIGHEST
    ) + time_bias.astype(jnp.float32)
    per_token = jnp.dot(onehot, per_seq, precision=lax.Precision.HIGHEST)
    return (per_token[:, :width], per_token[:, width : 2 * width], per_token[:, 2 * width :])


def modnorm(middle, scale, shift):
    return normalize(middle) * (1.0 + scale) + shift


def forward(entering, weights, table):
    (
        gain,
        attend_in,
        attend_out,
        time_weight,
        time_bias,
        expand_weight,
        expand_bias,
        reduce_weight,
        reduce_bias,
    ) = weights
    onehot, place, same, embed = table
    span, width = entering.shape
    inputs = entering.astype(jnp.float32)
    normed16 = (normalize(inputs) * gain.astype(jnp.float32)).astype(jnp.bfloat16)
    joint = jnp.dot(normed16, attend_in, preferred_element_type=jnp.float32)
    cos_part, sin_part = angles(place)
    query = joint[:, :width].reshape(span, HEADS, HEAD) * 0.125
    query16 = rotate(query, cos_part, sin_part).astype(jnp.bfloat16)
    key16 = rotate(
        joint[:, width : 2 * width].reshape(span, HEADS, HEAD), cos_part, sin_part
    ).astype(jnp.bfloat16)
    value16 = joint[:, 2 * width :].reshape(span, HEADS, HEAD).astype(jnp.bfloat16)
    scores = jnp.einsum("thd,uhd->htu", query16, key16, preferred_element_type=jnp.float32)
    scores = jnp.where(same[None], scores, -1e30)
    probs = jax.nn.softmax(scores, axis=-1)
    mixed16 = (
        jnp.einsum(
            "htu,uhd->thd", probs.astype(jnp.bfloat16), value16, preferred_element_type=jnp.float32
        )
        .reshape(span, width)
        .astype(jnp.bfloat16)
    )
    middle = inputs + jnp.dot(mixed16, attend_out, preferred_element_type=jnp.float32)
    scale, shift, gate = modulation(time_weight, time_bias, onehot, embed, width)
    modded16 = modnorm(middle, scale, shift).astype(jnp.bfloat16)
    preact = jnp.dot(
        modded16, expand_weight, preferred_element_type=jnp.float32
    ) + expand_bias.astype(jnp.float32)
    active16 = jax.nn.gelu(preact, approximate=False).astype(jnp.bfloat16)
    branch = jnp.dot(
        active16, reduce_weight, preferred_element_type=jnp.float32
    ) + reduce_bias.astype(jnp.float32)
    result = middle + gate * branch
    return (
        result,
        (
            entering,
            normed16,
            query16,
            key16,
            value16,
            probs,
            mixed16,
            middle,
            modded16,
            preact,
            active16,
            branch,
        ),
    )


def input_chain(cotan, saved, weights, table):
    (
        gain,
        attend_in,
        attend_out,
        time_weight,
        time_bias,
        expand_weight,
        expand_bias,
        reduce_weight,
        reduce_bias,
    ) = weights
    (
        entering,
        normed16,
        query16,
        key16,
        value16,
        probs,
        mixed16,
        middle,
        modded16,
        preact,
        active16,
        branch,
    ) = saved
    onehot, place, same, embed = table
    span, width = entering.shape
    scale, shift, gate = modulation(time_weight, time_bias, onehot, embed, width)
    branch_grad = (cotan * gate).astype(jnp.bfloat16)
    gate_grad = cotan * branch
    grad_rbias = jnp.sum(branch_grad.astype(jnp.float32), axis=0)
    active_grad = jnp.einsum(
        "td,fd->tf", branch_grad, reduce_weight, preferred_element_type=jnp.float32
    ).astype(jnp.bfloat16)
    gelu_out, gelu_pull = jax.vjp(partial(jax.nn.gelu, approximate=False), preact)
    preact_grad = gelu_pull(active_grad.astype(jnp.float32))[0].astype(jnp.bfloat16)
    grad_ebias = jnp.sum(preact_grad.astype(jnp.float32), axis=0)
    modded_grad = (
        jnp.einsum("tf,df->td", preact_grad, expand_weight, preferred_element_type=jnp.float32)
        .astype(jnp.bfloat16)
        .astype(jnp.float32)
    )
    mod_out, mod_pull = jax.vjp(modnorm, middle, scale, shift)
    middle_part, scale_grad, shift_grad = mod_pull(modded_grad)
    middle_grad = cotan + middle_part
    token_grad = jnp.concatenate([scale_grad, shift_grad, gate_grad], axis=1)
    seq_grad = jnp.dot(onehot.T, token_grad, precision=lax.Precision.HIGHEST)
    grad_tbias = jnp.sum(seq_grad, axis=0)
    attn_grad = middle_grad.astype(jnp.bfloat16)
    mixed_grad = (
        jnp.einsum("te,de->td", attn_grad, attend_out, preferred_element_type=jnp.float32)
        .astype(jnp.bfloat16)
        .reshape(span, HEADS, HEAD)
    )
    prob_grad = (
        jnp.einsum("thd,uhd->htu", mixed_grad, value16, preferred_element_type=jnp.float32)
        .astype(jnp.bfloat16)
        .astype(jnp.float32)
    )
    value_grad = jnp.einsum(
        "htu,thd->uhd", probs.astype(jnp.bfloat16), mixed_grad, preferred_element_type=jnp.float32
    ).astype(jnp.bfloat16)
    score_grad = probs * (prob_grad - jnp.sum(probs * prob_grad, axis=-1, keepdims=True))
    score_grad = jnp.where(same[None], score_grad, 0.0).astype(jnp.bfloat16)
    query_grad = (
        jnp.einsum("htu,uhd->thd", score_grad, key16, preferred_element_type=jnp.float32)
        .astype(jnp.bfloat16)
        .astype(jnp.float32)
    )
    key_grad = (
        jnp.einsum("htu,thd->uhd", score_grad, query16, preferred_element_type=jnp.float32)
        .astype(jnp.bfloat16)
        .astype(jnp.float32)
    )
    cos_part, sin_part = angles(place)
    rot_out, rot_pull = jax.vjp(lambda values: rotate(values, cos_part, sin_part), query_grad)
    query_grad = rot_pull(query_grad)[0] * 0.125
    key_grad = rot_pull(key_grad)[0]
    joint_grad = jnp.concatenate(
        [
            query_grad.reshape(span, width),
            key_grad.reshape(span, width),
            value_grad.astype(jnp.float32).reshape(span, width),
        ],
        axis=1,
    ).astype(jnp.bfloat16)
    normed_grad = (
        jnp.einsum("te,de->td", joint_grad, attend_in, preferred_element_type=jnp.float32)
        .astype(jnp.bfloat16)
        .astype(jnp.float32)
    )
    norm_out, norm_pull = jax.vjp(
        lambda values, scaler: normalize(values) * scaler,
        entering.astype(jnp.float32),
        gain.astype(jnp.float32),
    )
    input_part, grad_gain = norm_pull(normed_grad)
    input_grad = middle_grad + input_part
    small_terms = (grad_gain, grad_tbias, grad_ebias, grad_rbias)
    operands = (
        active16,
        branch_grad,
        modded16,
        preact_grad,
        mixed16,
        attn_grad,
        normed16,
        joint_grad,
        seq_grad,
    )
    return (input_grad, small_terms, operands)


def weight_products(operands, embed):
    (
        active16,
        branch_grad,
        modded16,
        preact_grad,
        mixed16,
        attn_grad,
        normed16,
        joint_grad,
        seq_grad,
    ) = operands
    grad_rweight = jnp.einsum(
        "tf,td->fd", active16, branch_grad, preferred_element_type=jnp.float32
    )
    grad_eweight = jnp.einsum(
        "td,tf->df", modded16, preact_grad, preferred_element_type=jnp.float32
    )
    grad_oweight = jnp.einsum("td,te->de", mixed16, attn_grad, preferred_element_type=jnp.float32)
    grad_iweight = jnp.einsum("td,te->de", normed16, joint_grad, preferred_element_type=jnp.float32)
    grad_tweight = jnp.dot(embed.T, seq_grad, precision=lax.Precision.HIGHEST)
    return (grad_iweight, grad_oweight, grad_tweight, grad_eweight, grad_rweight)


def add_small(grads, small_terms):
    grad_gain, grad_tbias, grad_ebias, grad_rbias = small_terms
    return (
        grads[0] + grad_gain,
        grads[1],
        grads[2],
        grads[3],
        grads[4] + grad_tbias,
        grads[5],
        grads[6] + grad_ebias,
        grads[7],
        grads[8] + grad_rbias,
    )


def add_large(grads, large_terms):
    grad_iweight, grad_oweight, grad_tweight, grad_eweight, grad_rweight = large_terms
    return (
        grads[0],
        grads[1] + grad_iweight,
        grads[2] + grad_oweight,
        grads[3] + grad_tweight,
        grads[4],
        grads[5] + grad_eweight,
        grads[6],
        grads[7] + grad_rweight,
        grads[8],
    )


def pick(tree, slot):
    return jax.tree.map(
        lambda array: lax.dynamic_index_in_dim(array, slot, 0, keepdims=False), tree
    )


def place_at(tree, items, slot):
    return jax.tree.map(
        lambda array, item: lax.dynamic_update_index_in_dim(array, item, slot, 0), tree, items
    )


def per_device(
    ends_in,
    lengths,
    times,
    norm_gain,
    attend_in,
    attend_out,
    time_weight,
    time_bias,
    expand_weight,
    expand_bias,
    reduce_weight,
    reduce_bias,
):
    weights = tuple(
        (
            piece[0]
            for piece in (
                norm_gain,
                attend_in,
                attend_out,
                time_weight,
                time_bias,
                expand_weight,
                expand_bias,
                reduce_weight,
                reduce_bias,
            )
        )
    )
    local = ends_in[0]
    micro = lengths.shape[1]
    width = local.shape[1]
    span = local.shape[0] // micro
    section = lax.axis_index("section")
    leading = section == 0
    tables = jax.vmap(partial(segment_table, span=span))(lengths[0], times[0])
    outputs = jnp.zeros((micro, span, width), jnp.bfloat16)
    stash = (jnp.zeros((micro, span, width), jnp.bfloat16),)
    arrived = jnp.zeros((span, width), jnp.bfloat16)
    for moment in range(micro + 1):
        turn = moment - section
        running = (turn >= 0) & (turn < micro)
        slot = jnp.clip(turn, 0, micro - 1)
        own_rows = lax.dynamic_slice_in_dim(local, slot * span, span, 0)
        entering = jnp.where(leading, own_rows, arrived)

        def advance(state, entering=entering, slot=slot):
            result, saved = forward(entering, weights, pick(tables, slot))
            kept = (entering,)
            return (
                lax.dynamic_update_index_in_dim(state[0], result.astype(jnp.bfloat16), slot, 0),
                place_at(state[1], kept, slot),
            )

        outputs, stash = lax.cond(running, advance, lambda state: state, (outputs, stash))
        if moment < micro:
            leaving = lax.dynamic_index_in_dim(outputs, slot, 0, keepdims=False)
            arrived = from_behind(leaving, "section", 1)
    grads = tuple((jnp.zeros(piece.shape, jnp.float32) for piece in weights))
    returned = jnp.zeros((micro, span, width), jnp.bfloat16)
    pending = ()

    def retreat(state, cotan, slot):
        table = pick(tables, slot)
        saved = forward(pick(stash, slot)[0], weights, table)[1]
        input_grad, small_terms, operands = input_chain(cotan, saved, weights, table)
        totals = add_small(state[1], small_terms)
        totals = add_large(totals, weight_products(operands, table[3]))
        waiting = state[2]
        return (
            lax.dynamic_update_index_in_dim(state[0], input_grad.astype(jnp.bfloat16), slot, 0),
            totals,
            waiting,
        )

    arrived = jnp.zeros((span, width), jnp.bfloat16)
    for moment in range(micro + 1):
        turn = moment - 1 + section
        running = (turn >= 0) & (turn < micro)
        slot = jnp.clip(turn, 0, micro - 1)
        own_rows = lax.dynamic_slice_in_dim(local, slot * span, span, 0)
        cotan = jnp.where(leading, arrived, own_rows).astype(jnp.float32)
        returned, grads, pending = lax.cond(
            running,
            partial(retreat, cotan=cotan, slot=slot),
            lambda state: state,
            (returned, grads, pending),
        )
        if moment < micro:
            leaving = lax.dynamic_index_in_dim(returned, slot, 0, keepdims=False)
            arrived = from_behind(leaving, "section", -1)
    ends_out = jnp.where(leading, returned, outputs).reshape(1, micro * span, width)
    shares = (
        lax.psum_scatter(grads[0], "rep", scatter_dimension=0, tiled=True),
        lax.psum_scatter(grads[1], "rep", scatter_dimension=0, tiled=True),
        lax.psum_scatter(grads[2], "rep", scatter_dimension=0, tiled=True),
        lax.psum_scatter(grads[3], "rep", scatter_dimension=0, tiled=True),
        lax.psum_scatter(grads[4], "rep", scatter_dimension=0, tiled=True),
        lax.psum_scatter(grads[5], "rep", scatter_dimension=0, tiled=True),
        lax.psum_scatter(grads[6], "rep", scatter_dimension=0, tiled=True),
        lax.psum_scatter(grads[7], "rep", scatter_dimension=0, tiled=True),
        lax.psum_scatter(grads[8], "rep", scatter_dimension=0, tiled=True),
    )
    results = [piece[None] for piece in shares]
    return (
        ends_out,
        results[0],
        results[1],
        results[2],
        results[3],
        results[4],
        results[5],
        results[6],
        results[7],
        results[8],
    )


def solution(mesh):
    return jax.shard_map(
        per_device,
        mesh=mesh,
        in_specs=(
            P("section", "rep", None),
            P("rep", None, None),
            P("rep", None, None),
            P("section", None),
            P("section", None, None),
            P("section", None, None),
            P("section", None, None),
            P("section", None),
            P("section", None, None),
            P("section", None),
            P("section", None, None),
            P("section", None),
        ),
        out_specs=(
            P("section", "rep", None),
            P("section", "rep"),
            P("section", "rep", None),
            P("section", "rep", None),
            P("section", "rep", None),
            P("section", "rep"),
            P("section", "rep", None),
            P("section", "rep"),
            P("section", "rep", None),
            P("section", "rep"),
        ),
        check_vma=False,
    )
```

profile of v0, /device:TPU:0, one launch (start us, length us, event | category | flops | bytes accessed | tf_op | source)
XLA Modules:
  0.0 941.3 jit_solution(6986432494975724465)
XLA Ops:
  17.7 40.8 %conditional.6 = (bf16[2,256,768]{2,1,0:T(8,128)(2,1)}, bf16[2,256,768]{2,1,0:T(8,128)(2,1)}) conditional(s32[]{:T(128)} %convert_element_type.604, () %tuple.54, (bf16[256,768]{1,0:T(8,128)(2,1)S(1)}, bf16[768]{0:T(1024)(128)(2,1)}, bf16[768,2304]{1,0:T(8,128)(2,1)}, s32[]{:T(128)}, pred[2,256,256]{1,2,0:T(8,128)(4,1)}, ...), branch_computations={%region_3.4_spmd, %region_4.11_spmd} | conditional | flops 3933168128 | bytes 71689232 | solution.py:374
  18.9 3.1 fusion.47
  27.9 2.5 fusion.628
  35.6 3.5 fusion.65
  40.1 14.7 %fusion.35 = bf16[2,256,768]{2,1,0:T(8,128)(2,1)} fusion(bf16[2,256,768]{2,1,0:T(8,128)(2,1)} %broadcast.1099.clone, s32[]{:T(128)S(6)} %select_n.131, f32[256,768]{1,0:T(8,128)S(1)} %get-tuple-element.644, bf16[3072,768]{1,0:T(8,128)(2,1)} %get-tuple-element.413, f32[3072]{0:T(1024)S(1)} %convert_element_type.438, ...), kind=kOutput, calls=%fused_computation.37 | convolution fusion | flops 2469789696 | bytes 13780996 | tf_op jit(solution)/shard_map/cond/branch_1_fun/dot_general | solution.py:116
  60.9 9.2 collective-permute-done
  70.3 36.6 %conditional.7 = ((bf16[2,256,768]{2,1,0:T(8,128)(2,1)}, bf16[2,256,768]{2,1,0:T(8,128)(2,1)})) conditional(s32[]{:T(128)} %convert_element_type.603, (bf16[2,256,768]{2,1,0:T(8,128)(2,1)}, bf16[2,256,768]{2,1,0:T(8,128)(2,1)}) %conditional.6, (bf16[256,768]{1,0:T(8,128)(2,1)S(1)}, bf16[768]{0:T(1024)(128)(2,1)}, bf16[768,2304]{1,0:T(8,128)(2,1)}, ...), branch_computations={%region_11.12_spmd, %region_12.19_spmd} | conditional | flops 3933168128 | bytes 70116376 | solution.py:374
  71.4 3.1 fusion.152
  88.1 3.5 fusion.170
  91.6 14.4 %fusion.140 = bf16[2,256,768]{2,1,0:T(8,128)(2,1)} fusion(bf16[2,256,768]{2,1,0:T(8,128)(2,1)} %get-tuple-element.415, s32[]{:T(128)S(6)} %select_n.133, f32[256,768]{1,0:T(8,128)S(1)} %get-tuple-element.658, bf16[3072,768]{1,0:T(8,128)(2,1)} %get-tuple-element.429, f32[3072]{0:T(1024)S(1)} %convert_element_type.452, ...), kind=kOutput, calls=%fused_computation.156 | convolution fusion | flops 2469789696 | bytes 13780996 | tf_op jit(solution)/shard_map/cond/branch_1_fun/dot_general | solution.py:116
  107.8 4.6 collective-permute-start.1
  112.5 8.4 collective-permute-done.1
  120.9 7.8 conditional.8
  128.6 25.1 %conditional.9 = (bf16[2,256,768]{2,1,0:T(8,128)(2,1)}, f32[768]{0:T(1024)}, f32[768,2304]{1,0:T(8,128)}, f32[768,768]{1,0:T(8,128)}, f32[128,2304]{1,0:T(8,128)...) conditional(s32[]{:T(128)} %convert_element_type.601, () %tuple.53, ...), branch_computations={%region_27.28_spmd, %region_28.44_spmd} | conditional | flops 11680322560 | bytes 235363216 | solution.py:402
  128.7 4.8 broadcast_in_dim.247
  133.5 4.3 broadcast_in_dim.249
  137.7 3.3 broadcast_in_dim.243
  156.0 105.4 %collective-permute-done.2 = bf16[256,768]{1,0:T(8,128)(2,1)S(1)} collective-permute-done((bf16[256,768]{1,0:T(8,128)(2,1)S(1)}, bf16[256,768]{1,0:T(8,128)(2,1)S(1)}, u32[]{:S(2)}, u32[]{:S(2)}) %collective-permute-start.2) | collective-permute-done | bytes 393248 | tf_op jit(solution)/shard_map/ppermute | solution.py:18
  262.6 104.4 %conditional.10 = ((bf16[2,256,768]{2,1,0:T(8,128)(2,1)}, f32[768]{0:T(1024)}, f32[768,2304]{1,0:T(8,128)}, f32[768,768]{1,0:T(8,128)}, f32[128,2304]{1,0:T(8,12...) conditional(s32[]{:T(128)} %convert_element_type.600, ...), branch_computations={%region_44.45_spmd, %region_45.61_spmd} | conditional | flops 11687702528 | bytes 264212448 | solution.py:402
  265.7 3.3 fusion.513
  278.3 4.5 fusion.639
  290.9 9.5 %multiply_convert_fusion.2 = (bf16[256,3072]{1,0:T(8,128)(2,1)S(1)}, f32[256,3072]{1,0:T(8,128)S(1)}, f32[256,3072]{1,0:T(8,128)S(1)}) fusion(f32[3072]{0:T(1024)S(1)} %convert_element_type.519, bf16[256,768]{1,0:T(8,128)(2,1)S(1)} %get-tuple-element.706, bf16[768,3072]{1,0:T(8,128)(2,1)S(1)} %bitcast.508), kind=kOutput, calls=%fused_computation.549 | convolution fusion | flops 1259864064 | bytes 12988416 | tf_op jit(solution)/shard_map/cond/branch_1_fun/dot_general | solution.py:112
  300.4 2.7 convert_reduce_fusion.6
  303.1 8.8 convolution_add_fusion.15
  316.8 3.5 convolution_add_fusion.17
  320.2 8.8 convolution_add_fusion.14
  332.8 5.0 fusion.459
  337.9 5.1 fusion.456
  346.1 7.4 convolution_add_fusion.13
  353.5 3.7 convolution_add_fusion.19
  369.3 10.0 %collective-permute-done.3 = bf16[256,768]{1,0:T(8,128)(2,1)S(1)} collective-permute-done((bf16[256,768]{1,0:T(8,128)(2,1)S(1)}, bf16[256,768]{1,0:T(8,128)(2,1)S(1)}, u32[]{:S(2)}, u32[]{:S(2)}) %collective-permute-start.3) | collective-permute-done | bytes 393248 | tf_op jit(solution)/shard_map/ppermute | solution.py:18
  380.4 104.4 %conditional.11 = ((bf16[2,256,768]{2,1,0:T(8,128)(2,1)}, f32[768]{0:T(1024)}, f32[768,2304]{1,0:T(8,128)}, f32[768,768]{1,0:T(8,128)}, f32[128,2304]{1,0:T(8,12...) conditional(s32[]{:T(128)} %convert_element_type.599, ...), branch_computations={%region_61.62_spmd, %region_62.78_spmd} | conditional | flops 11687702528 | bytes 264200128 | solution.py:402
  383.9 3.3 fusion.612
  396.5 4.4 fusion.642
  408.5 9.5 %multiply_convert_fusion.4 = (bf16[256,3072]{1,0:T(8,128)(2,1)S(1)}, f32[256,3072]{1,0:T(8,128)S(1)}, f32[256,3072]{1,0:T(8,128)S(1)}) fusion(f32[3072]{0:T(1024)S(1)} %convert_element_type.557, bf16[256,768]{1,0:T(8,128)(2,1)S(1)} %get-tuple-element.739, bf16[768,3072]{1,0:T(8,128)(2,1)S(1)} %bitcast.510), kind=kOutput, calls=%fused_computation.716 | convolution fusion | flops 1259864064 | bytes 12988416 | tf_op jit(solution)/shard_map/cond/branch_1_fun/dot_general | solution.py:112
  418.0 2.7 convert_reduce_fusion.9
  420.8 8.8 convolution_add_fusion.24
  434.4 3.5 convolution_add_fusion.26
  437.9 8.8 convolution_add_fusion.23
  450.5 5.0 fusion.558
  455.5 5.1 fusion.555
  463.8 7.4 convolution_add_fusion.22
  471.2 3.7 convolution_add_fusion.28
  490.1 58.4 %all-reduce.16 = (f32[768]{0:T(1024)S(1)}, f32[2304]{0:T(1024)S(1)}, f32[3072]{0:T(1024)S(1)}, f32[768]{0:T(1024)S(1)}) all-reduce(f32[768]{0:T(1024)} %get-tuple-element.592, f32[2304]{0:T(1024)} %get-tuple-element.596, f32[3072]{0:T(1024)} %get-tuple-element.598, ...), channel_id=2, replica_groups=mesh['section'=2,'rep'=16] {'rep'}, use_global_device_ids=true, to_apply=%region_78.79.clone | all-reduce | flops 6912 | bytes 55296
  552.5 56.2 %reduce-scatter.8.cloned.1.call-done = f32[48,768]{1,0:T(8,128)} async-done(((f32[768,768]{1,0:T(8,128)}), f32[48,768]{1,0:T(8,128)}) %reduce-scatter.8.cloned.1.call-update) | async-done | bytes 147472 | tf_op jit(solution)/shard_map/reduce_scatter | solution.py:415
  608.7 94.2 %reduce-scatter.6.cloned.1.call-done = f32[48,2304]{1,0:T(8,128)} async-done(((f32[768,2304]{1,0:T(8,128)}), f32[48,2304]{1,0:T(8,128)}) %reduce-scatter.6.cloned.1.call-update) | async-done | bytes 442384 | tf_op jit(solution)/shard_map/reduce_scatter | solution.py:414
  702.9 115.4 %reduce-scatter.12.cloned.1.call-done = f32[48,3072]{1,0:T(8,128)} async-done(((f32[768,3072]{1,0:T(8,128)}), f32[48,3072]{1,0:T(8,128)}) %reduce-scatter.12.cloned.1.call-update) | async-done | bytes 589840 | tf_op jit(solution)/shard_map/reduce_scatter | solution.py:418
  818.3 116.2 %reduce-scatter.14.cloned.1.call-done = f32[192,768]{1,0:T(8,128)} async-done(((f32[3072,768]{1,0:T(8,128)}), f32[192,768]{1,0:T(8,128)}) %reduce-scatter.14.cloned.1.call-update) | async-done | bytes 589840 | tf_op jit(solution)/shard_map/reduce_scatter | solution.py:420
  (378 shorter events, 146.7 us)
Async XLA Ops:
  7.2 545.3 %reduce-scatter.10.cloned.1.call-start = ((), (), s32[]{:S(2)}) async-start(), calls=%async_computation.7 | async-start | bytes 1253376 | tf_op jit(solution)/shard_map/reduce_scatter | solution.py:416
  17.7 52.4 %copy-start.24 = (bf16[1,512,768]{2,1,0:T(8,128)(2,1)S(1)}, bf16[1,512,768]{2,1,0:T(8,128)(2,1)}, u32[]{:S(2)}) copy-start(bf16[1,512,768]{2,1,0:T(8,128)(2,1)} %param.24) | copy-start | bytes 2359300
  34.3 4.9 copy-start.76
  59.6 10.6 %collective-permute-start = (bf16[256,768]{1,0:T(8,128)(2,1)S(1)}, bf16[256,768]{1,0:T(8,128)(2,1)S(1)}, u32[]{:S(2)}, u32[]{:S(2)}) collective-permute-start(bf16[256,768]{1,0:T(8,128)(2,1)S(1)} %dynamic-slice_bitcast_fusion.9), channel_id=1, source_target_pairs={{0,16},{1,17},{2,18},{3,19},{4,20},{5,21},{6,22},{7,23},{8,24},{9,... | collective-permute-start | bytes 1179656 | tf_op jit(solution)/shard_map/ppermute | solution.py:18
  86.8 4.9 copy-start.77
  107.8 13.0 %collective-permute-start.1 = (bf16[256,768]{1,0:T(8,128)(2,1)S(1)}, bf16[256,768]{1,0:T(8,128)(2,1)S(1)}, u32[]{:S(2)}, u32[]{:S(2)}) collective-permute-start(bf16[256,768]{1,0:T(8,128)(2,1)S(1)} %dynamic-slice_bitcast_fusion.8), channel_id=1, source_target_pairs={{0,16},{1,17},{2,18},{3,19},{4,20},{5,21},{6,22},{7,23},{8,24},{9,... | collective-permute-start | bytes 1179656 | tf_op jit(solution)/shard_map/ppermute | solution.py:18
  154.7 106.7 %collective-permute-start.2 = (bf16[256,768]{1,0:T(8,128)(2,1)S(1)}, bf16[256,768]{1,0:T(8,128)(2,1)S(1)}, u32[]{:S(2)}, u32[]{:S(2)}) collective-permute-start(bf16[256,768]{1,0:T(8,128)(2,1)S(1)} %dynamic-slice_bitcast_fusion.7), channel_id=1, source_target_pairs={{16,0},{17,1},{18,2},{19,3},{20,4},{21,5},{22,6},{23,7},{24,8},{25... | collective-permute-start | bytes 1179656 | tf_op jit(solution)/shard_map/ppermute | solution.py:18
  263.7 5.3 copy-start.87
  269.0 5.9 copy-start.98
  270.3 7.3 copy-start.29
  275.2 7.5 copy-start.31
  275.2 7.5 copy-start.33
  277.6 5.1 copy-start.49
  283.0 7.9 slice-start.2
  285.5 5.4 slice-start.3
  289.9 10.5 %slice-start.8 = ((s8[4718592]{0:T(1024)(128)(4,1)}), s8[4194304]{0:T(1024)(128)(4,1)S(1)}, s32[]{:S(2)}) async-start(s8[4718592]{0:T(1024)(128)(4,1)} %bitcast.519), calls=%async_computation.18 | async-start | bytes 8388608 | tf_op jit(solution)/shard_map/cond
  290.9 9.5 %slice-start.9 = ((s8[4718592]{0:T(1024)(128)(4,1)}), s8[524288]{0:T(1024)(128)(4,1)S(1)}, s32[]{:S(2)}) async-start(s8[4718592]{0:T(1024)(128)(4,1)} %bitcast.519), calls=%async_computation.19 | async-start | bytes 1048576 | tf_op jit(solution)/shard_map/cond
  332.8 5.1 copy-start.50
  332.8 5.1 copy-start.51
  332.8 5.0 copy-start.82
  332.8 5.0 copy-start.113
  337.9 5.2 copy-start.32
  337.9 5.2 copy-start.34
  346.1 7.4 copy-start.18
  359.5 4.8 copy-start.101
  359.5 6.2 copy-start.100
  368.0 11.3 %collective-permute-start.3 = (bf16[256,768]{1,0:T(8,128)(2,1)S(1)}, bf16[256,768]{1,0:T(8,128)(2,1)S(1)}, u32[]{:S(2)}, u32[]{:S(2)}) collective-permute-start(bf16[256,768]{1,0:T(8,128)(2,1)S(1)} %dynamic-slice_bitcast_fusion.6), channel_id=1, source_target_pairs={{16,0},{17,1},{18,2},{19,3},{20,4},{21,5},{22,6},{23,7},{24,8},{25... | collective-permute-start | bytes 1179656 | tf_op jit(solution)/shard_map/ppermute | solution.py:18
  381.9 5.3 copy-start.89
  387.2 5.9 copy-start.99
  388.5 7.3 copy-start.30
  393.4 7.5 copy-start.35
  393.4 7.5 copy-start.37
  395.8 5.1 copy-start.52
  401.2 7.3 slice-start.4
  403.7 4.8 slice-start.5
  408.1 9.9 %slice-start.10 = ((s8[4718592]{0:T(1024)(128)(4,1)}), s8[4194304]{0:T(1024)(128)(4,1)S(1)}, s32[]{:S(2)}) async-start(s8[4718592]{0:T(1024)(128)(4,1)} %bitcast.521), calls=%async_computation.20 | async-start | bytes 8388608 | tf_op jit(solution)/shard_map/cond
  408.5 9.5 %slice-start.11 = ((s8[4718592]{0:T(1024)(128)(4,1)}), s8[524288]{0:T(1024)(128)(4,1)S(1)}, s32[]{:S(2)}) async-start(s8[4718592]{0:T(1024)(128)(4,1)} %bitcast.521), calls=%async_computation.21 | async-start | bytes 1048576 | tf_op jit(solution)/shard_map/cond
  450.4 5.1 copy-start.53
  450.4 5.1 copy-start.54
  450.5 5.0 copy-start.83
  450.5 5.0 copy-start.114
  455.5 5.2 copy-start.36
  455.5 5.2 copy-start.38
  463.8 7.4 copy-start.20
  484.8 123.9 %reduce-scatter.8.cloned.1.call-start = ((), (), s32[]{:S(2)}) async-start(), calls=%async_computation.6 | async-start | bytes 2506752 | tf_op jit(solution)/shard_map/reduce_scatter | solution.py:415
  485.6 217.3 %reduce-scatter.6.cloned.1.call-start = ((), (), s32[]{:S(2)}) async-start(), calls=%async_computation.5 | async-start | bytes 7520256 | tf_op jit(solution)/shard_map/reduce_scatter | solution.py:414
  486.3 332.0 %reduce-scatter.12.cloned.1.call-start = ((), (), s32[]{:S(2)}) async-start(), calls=%async_computation.8 | async-start | bytes 10027008 | tf_op jit(solution)/shard_map/reduce_scatter | solution.py:418
  486.9 447.6 %reduce-scatter.14.cloned.1.call-start = ((), (), s32[]{:S(2)}) async-start(), calls=%async_computation.9 | async-start | bytes 10027008 | tf_op jit(solution)/shard_map/reduce_scatter | solution.py:420
  (48 other events, 92.0 us)
Sparse Core Ops, SparseCore 0:
  484.9 57.3 reduce-scatter.9
  546.7 61.9 reduce-scatter.7
  613.8 89.0 reduce-scatter.5
  707.4 110.8 reduce-scatter.11
  823.4 111.0 reduce-scatter.13
where the time goes:
time: 953 us; the launch traced here: 941 us
  waiting for transfers between devices  517 us (54%)
  matrix products  204 us (21%)
  other arithmetic  63.6 us (7%)
  blocking collectives  58.4 us (6%)
  local copies, waits for them, and re-layouts  54.3 us (6%)
  loops' own time  18.4 us (2%)
  between operations  16.2 us (2%)
    ppermute x4, waiting for transfers between devices, from_behind(): return lax.ppermute(block, axis, route)  133 us
    reduce_scatter x1, waiting for transfers between devices, per_device(): lax.psum_scatter(grads[7], 'rep', scatter_dimension=0, tiled=True)  116 us
    reduce_scatter x1, waiting for transfers between devices, per_device(): lax.psum_scatter(grads[5], 'rep', scatter_dimension=0, tiled=True)  115 us
    reduce_scatter x1, waiting for transfers between devices, per_device(): lax.psum_scatter(grads[1], 'rep', scatter_dimension=0, tiled=True)  94.2 us
    unnamed x1, blocking collectives  58.4 us
    reduce_scatter x1, waiting for transfers between devices, per_device(): lax.psum_scatter(grads[2], 'rep', scatter_dimension=0, tiled=True)  56.2 us
    dot_general x4, matrix products, forward(): jnp.dot(active16, reduce_weight, preferred_element_type=jnp.float32)  31.9 us
  transfers between devices with their start and end apart: 9, of which 8 were waited for; matrix products, arithmetic and copies ran while one was open for 0% of the time, Pallas kernels for 0%

commit v1 on v0

--- a/solution.py
+++ b/solution.py
@@ -273,47 +273,29 @@
     grad_tweight = jnp.dot(embed.T, seq_grad, precision=lax.Precision.HIGHEST)
     return (grad_iweight, grad_oweight, grad_tweight, grad_eweight, grad_rweight)
 
-
-def add_small(grads, small_terms):
-    grad_gain, grad_tbias, grad_ebias, grad_rbias = small_terms
-    return (
-        grads[0] + grad_gain,
-        grads[1],
-        grads[2],
-        grads[3],
-        grads[4] + grad_tbias,
-        grads[5],
-        grads[6] + grad_ebias,
-        grads[7],
-        grads[8] + grad_rbias,
-    )
-
-
-def add_large(grads, large_terms):
-    grad_iweight, grad_oweight, grad_tweight, grad_eweight, grad_rweight = large_terms
-    return (
-        grads[0],
-        grads[1] + grad_iweight,
-        grads[2] + grad_oweight,
-        grads[3] + grad_tweight,
-        grads[4],
-        grads[5] + grad_eweight,
-        grads[6],
-        grads[7] + grad_rweight,
-        grads[8],
-    )
-
-
-def pick(tree, slot):
-    return jax.tree.map(
-        lambda array: lax.dynamic_index_in_dim(array, slot, 0, keepdims=False), tree
-    )
-
-
-def place_at(tree, items, slot):
-    return jax.tree.map(
-        lambda array, item: lax.dynamic_update_index_in_dim(array, item, slot, 0), tree, items
-    )
+def bits_of(count):
+    bits = count.bit_length() - 1
+    assert 1 << bits == count
+    return bits
+
+
+def halve_sum(terms, axis, order):
+    count = terms.shape[0]
+    bits = bits_of(count)
+    me = lax.axis_index(axis)
+    view = terms.reshape((2,) * bits + terms.shape[1:])
+    left = list(range(bits - 1, -1, -1))
+    for step, bit in enumerate(order):
+        spot = left.index(bit)
+        own = (me >> bit) & 1
+        keep = lax.dynamic_index_in_dim(view, own, spot, keepdims=False)
+        send = lax.dynamic_index_in_dim(view, 1 - own, spot, keepdims=False)
+        came = lax.ppermute(send, axis, [(i, i ^ (1 << bit)) for i in range(count)])
+        view = keep.astype(jnp.float32) + came.astype(jnp.float32)
+        if step < bits - 1:
+            view = view.astype(jnp.bfloat16)
+        left.remove(bit)
+    return view
 
 
 def per_device(
@@ -348,91 +330,113 @@
     )
     local = ends_in[0]
     micro = lengths.shape[1]
+    assert micro == 2
     width = local.shape[1]
     span = local.shape[0] // micro
     section = lax.axis_index("section")
     leading = section == 0
-    tables = jax.vmap(partial(segment_table, span=span))(lengths[0], times[0])
-    outputs = jnp.zeros((micro, span, width), jnp.bfloat16)
-    stash = (jnp.zeros((micro, span, width), jnp.bfloat16),)
-    arrived = jnp.zeros((span, width), jnp.bfloat16)
-    for moment in range(micro + 1):
-        turn = moment - section
-        running = (turn >= 0) & (turn < micro)
-        slot = jnp.clip(turn, 0, micro - 1)
-        own_rows = lax.dynamic_slice_in_dim(local, slot * span, span, 0)
-        entering = jnp.where(leading, own_rows, arrived)
-
-        def advance(state, entering=entering, slot=slot):
-            result, saved = forward(entering, weights, pick(tables, slot))
-            kept = (entering,)
-            return (
-                lax.dynamic_update_index_in_dim(state[0], result.astype(jnp.bfloat16), slot, 0),
-                place_at(state[1], kept, slot),
-            )
-
-        outputs, stash = lax.cond(running, advance, lambda state: state, (outputs, stash))
-        if moment < micro:
-            leaving = lax.dynamic_index_in_dim(outputs, slot, 0, keepdims=False)
-            arrived = from_behind(leaving, "section", 1)
-    grads = tuple((jnp.zeros(piece.shape, jnp.float32) for piece in weights))
-    returned = jnp.zeros((micro, span, width), jnp.bfloat16)
-    pending = ()
-
-    def retreat(state, cotan, slot):
-        table = pick(tables, slot)
-        saved = forward(pick(stash, slot)[0], weights, table)[1]
-        input_grad, small_terms, operands = input_chain(cotan, saved, weights, table)
-        totals = add_small(state[1], small_terms)
-        totals = add_large(totals, weight_products(operands, table[3]))
-        waiting = state[2]
+    tables = [segment_table(lengths[0, slot], times[0, slot], span) for slot in range(micro)]
+    rows = [local[slot * span : (slot + 1) * span] for slot in range(micro)]
+
+    def first_half(slot, entering):
+        return forward(entering, weights, tables[slot])[0].astype(jnp.bfloat16)
+
+    def both_halves(slot, entering, cotan):
+        result, saved = forward(entering, weights, tables[slot])
+        input_grad, small_terms, operands = input_chain(
+            cotan.astype(jnp.float32), saved, weights, tables[slot]
+        )
         return (
-            lax.dynamic_update_index_in_dim(state[0], input_grad.astype(jnp.bfloat16), slot, 0),
-            totals,
-            waiting,
+            result.astype(jnp.bfloat16),
+            input_grad.astype(jnp.bfloat16),
+            small_terms,
+            operands,
         )
 
-    arrived = jnp.zeros((span, width), jnp.bfloat16)
-    for moment in range(micro + 1):
-        turn = moment - 1 + section
-        running = (turn >= 0) & (turn < micro)
-        slot = jnp.clip(turn, 0, micro - 1)
-        own_rows = lax.dynamic_slice_in_dim(local, slot * span, span, 0)
-        cotan = jnp.where(leading, arrived, own_rows).astype(jnp.float32)
-        returned, grads, pending = lax.cond(
-            running,
-            partial(retreat, cotan=cotan, slot=slot),
-            lambda state: state,
-            (returned, grads, pending),
-        )
-        if moment < micro:
-            leaving = lax.dynamic_index_in_dim(returned, slot, 0, keepdims=False)
-            arrived = from_behind(leaving, "section", -1)
-    ends_out = jnp.where(leading, returned, outputs).reshape(1, micro * span, width)
-    shares = (
-        lax.psum_scatter(grads[0], "rep", scatter_dimension=0, tiled=True),
-        lax.psum_scatter(grads[1], "rep", scatter_dimension=0, tiled=True),
-        lax.psum_scatter(grads[2], "rep", scatter_dimension=0, tiled=True),
-        lax.psum_scatter(grads[3], "rep", scatter_dimension=0, tiled=True),
-        lax.psum_scatter(grads[4], "rep", scatter_dimension=0, tiled=True),
-        lax.psum_scatter(grads[5], "rep", scatter_dimension=0, tiled=True),
-        lax.psum_scatter(grads[6], "rep", scatter_dimension=0, tiled=True),
-        lax.psum_scatter(grads[7], "rep", scatter_dimension=0, tiled=True),
-        lax.psum_scatter(grads[8], "rep", scatter_dimension=0, tiled=True),
-    )
-    results = [piece[None] for piece in shares]
-    return (
-        ends_out,
-        results[0],
-        results[1],
-        results[2],
-        results[3],
-        results[4],
-        results[5],
-        results[6],
-        results[7],
-        results[8],
-    )
+    shapes = jax.eval_shape(lambda a, b: both_halves(0, a, b), rows[0], rows[0])
+    blank = jax.tree.map(lambda s: jnp.zeros(s.shape, s.dtype), shapes)
+    swap = [(0, 1), (1, 0)]
+    out0 = lax.cond(
+        leading, lambda: first_half(0, rows[0]), lambda: jnp.zeros((span, width), jnp.bfloat16)
+    )
+    came0 = lax.ppermute(out0, "section", [(0, 1)])
+    phase_b = lax.cond(
+        leading,
+        lambda: (blank[0], first_half(1, rows[1]), blank[2], blank[3]),
+        lambda: both_halves(0, came0, rows[0]),
+    )
+    came1 = lax.ppermute(phase_b[1], "section", swap)
+    pick0 = lambda a, b: jax.tree.map(lambda x, y: jnp.where(leading, x, y), a, b)
+    slot_tab = pick0(tables[0], tables[1])
+    result_c, saved = forward(jnp.where(leading, rows[0], came1), weights, slot_tab)
+    grad_c, small_c, operands_c = input_chain(
+        jnp.where(leading, came1, rows[1]).astype(jnp.float32), saved, weights, slot_tab
+    )
+    phase_c = (result_c.astype(jnp.bfloat16), grad_c.astype(jnp.bfloat16), small_c, operands_c)
+    came2 = lax.ppermute(phase_c[1], "section", [(1, 0)])
+    phase_d = lax.cond(
+        leading,
+        lambda: both_halves(1, rows[1], came2),
+        lambda: phase_b,
+    )
+    ends_out = jnp.where(
+        leading,
+        jnp.concatenate([phase_c[1], phase_d[1]]),
+        jnp.concatenate([phase_b[0], phase_c[0]]),
+    )[None]
+    small = jax.tree.map(lambda x, y: x + y, phase_c[2], phase_d[2])
+    operands = jax.tree.map(lambda x, y: jnp.concatenate([x, y]), phase_c[3], phase_d[3])
+    embed = jnp.concatenate(
+        [slot_tab[3], jnp.where(leading, tables[1][3], tables[0][3])]
+    )
+    grad_iweight, grad_oweight, grad_tweight, grad_eweight, grad_rweight = weight_products(
+        operands, embed
+    )
+    grad_gain, grad_tbias, grad_ebias, grad_rbias = small
+    count = lax.axis_size("rep")
+
+    def block(grad):
+        return grad.reshape((count, grad.shape[0] // count) + grad.shape[1:]).astype(jnp.bfloat16)
+
+    tail_parts = [
+        grad_oweight.reshape(count, -1, width),
+        grad_tweight.reshape(count, -1, width),
+    ]
+    smalls = jnp.concatenate(
+        [piece.reshape(count, -1) for piece in (grad_gain, grad_tbias, grad_ebias, grad_rbias)], 1
+    )
+    small_width = smalls.shape[1]
+    smalls = jnp.pad(smalls, ((0, 0), (0, width - small_width)))[:, None]
+    tail = jnp.concatenate(tail_parts + [smalls], axis=1)
+    pad = -tail.shape[1] % 16
+    tail = jnp.pad(tail, ((0, 0), (0, pad), (0, 0))).astype(jnp.bfloat16)
+    bits = bits_of(count)
+    plain = list(range(bits))
+    turned = plain if bits < 3 else [0, 2, 1] + plain[3:]
+    share_r = halve_sum(block(grad_rweight), "rep", plain)
+    share_e = halve_sum(block(grad_eweight), "rep", plain)
+    share_i = halve_sum(block(grad_iweight), "rep", turned)
+    share_t = halve_sum(tail, "rep", plain)
+    rows_o = width // count
+    rows_t = EMB // count
+    share_o = share_t[:rows_o]
+    share_w = share_t[rows_o : rows_o + 3 * rows_t].reshape(rows_t, 3 * width)
+    line = share_t[rows_o + 3 * rows_t]
+    cuts = [width // count, 3 * width // count, expand_bias.shape[1] // count, width // count]
+    spots = [sum(cuts[:i]) for i in range(5)]
+    share_gain, share_tb, share_eb, share_rb = (line[spots[i] : spots[i + 1]] for i in range(4))
+    results = (
+        share_gain,
+        share_i,
+        share_o,
+        share_w,
+        share_tb,
+        share_e,
+        share_eb,
+        share_r,
+        share_rb,
+    )
+    return (ends_out,) + tuple(piece[None] for piece in results)
 
 
 def solution(mesh):

time: 953 us -> 518 us (0.54); the launches traced: 941 us -> 517 us
  waiting for transfers between devices: 517 us -> 99.8 us
  starting transfers between devices: 8.74 us -> 87.3 us
  blocking collectives: 58.4 us -> 0 us
  matrix products: 204 us -> 179 us
  other arithmetic: 63.6 us -> 86.3 us
  between operations: 16.2 us -> 2.19 us
  loops' own time: 18.4 us -> 5.88 us
    reduce_scatter x5 -> x0, waiting for transfers between devices: 382 us -> none  [the longest x1 116 us: per_device(): lax.psum_scatter(grads[7], 'rep', scatter_dimension=0, tiled=True)]
    ppermute x4 -> x19, starting transfers between devices: 8.54 us -> 87.3 us  [the longest x1 68.9 us: per_device(): came1 = lax.ppermute(phase_b[1], 'section', swap)]
    unnamed x1 -> x0, blocking collectives: 58.4 us -> none
    ppermute x4 -> x19, waiting for transfers between devices: 133 us -> 99.8 us  [the longest x16 89.3 us: halve_sum(): came = lax.ppermute(send, axis, [(i, i ^ 1 << bit) for i in range(count)])]
    another operation x6 -> x2, loops' own time: 18.4 us -> 1.59 us  [the longest x1 0.98 us: per_device(): lax.cond(leading, lambda: both_halves(1, rows[1], came2), lambda: phase_b)]
    broadcast_in_dim x12 -> x6, local copies, waits for them, and re-layouts: 18.3 us -> 2.6 us  [the longest x4 1.89 us: per_device(): blank = jax.tree.map(lambda s: jnp.zeros(s.shape, s.dtype), shapes)]
    dot_general x2 -> x1, matrix products: 17.5 us -> 3.88 us  [weight_products(): jnp.einsum('td,tf->df', modded16, preact_grad, preferred_element_type=jnp...]
    dot_general x2 -> x1, matrix products: 17.7 us -> 4.17 us  [weight_products(): jnp.einsum('tf,td->fd', active16, branch_grad, preferred_element_type=jnp...]
  transfers between devices with their start and end apart: 9 -> 19, of which waited for: 8 -> 11; matrix products, arithmetic and copies ran while one was open for 0% -> 11% of each run, Pallas kernels for 0% -> 0%
where the time goes in v1:
time: 518 us; the launch traced here: 517 us
  matrix products  179 us (35%)
  waiting for transfers between devices  99.8 us (19%)
  starting transfers between devices  87.3 us (17%)
  other arithmetic  86.3 us (17%)
  local copies, waits for them, and re-layouts  56.6 us (11%)
  loops' own time  5.88 us (1%)
    ppermute x16, waiting for transfers between devices, halve_sum(): came = lax.ppermute(send, axis, [(i, i ^ 1 << bit) for i in range(count)])  89.3 us
    ppermute x1, starting transfers between devices, per_device(): came1 = lax.ppermute(phase_b[1], 'section', swap)  68.9 us
    dot_general x4, matrix products, forward(): jnp.dot(active16, reduce_weight, preferred_element_type=jnp.float32)  32.6 us
    dot_general x2, matrix products, forward(): jnp.dot(modded16, expand_weight, preferred_element_type=jnp.float32)  18.6 us
    dot_general x4, matrix products, modulation(): per_token = jnp.dot(onehot, per_seq, precision=lax.Precision.HIGHEST)  16.7 us
    ppermute x16, starting transfers between devices, halve_sum(): came = lax.ppermute(send, axis, [(i, i ^ 1 << bit) for i in range(count)])  15.7 us
    dot_general x2, matrix products, input_chain(): jnp.einsum('htu,uhd->thd', score_grad, key16, preferred_element_type=jnp....  12 us
    dot_general x2, matrix products, input_chain(): jnp.einsum('htu,thd->uhd', score_grad, query16, preferred_element_type=jn...  12 us
  transfers between devices with their start and end apart: 19, of which 11 were waited for; matrix products, arithmetic and copies ran while one was open for 11% of the time, Pallas kernels for 0%

profile of v1, /device:TPU:0, one launch (start us, length us, event | category | flops | bytes accessed | tf_op | source)
XLA Modules:
  0.0 516.6 jit_solution(9797779523658808576)
XLA Ops:
  13.4 33.6 %conditional.5 = (bf16[256,768]{1,0:T(8,128)(2,1)S(1)}) conditional(s32[]{:T(128)} %convert_element_type.739, () %tuple.42, (bf16[256,768]{1,0:T(8,128)(2,1)}, bf16[768]{0:T(1024)(128)(2,1)}, bf16[768,2304]{1,0:T(8,128)(2,1)}, pred[256,256]{0,1:T(8,128)(4,1)}, f32[256]{0:T(256)}, /*index=5*/bf16[768,768]{1,0:T(8,128)(2,1)}, f32[4,128]{1,0:T(4,128)}, ...), branch_computations={%region_3.4_spmd, %region_4.11_spmd} | conditional | flops 3933168128 | bytes 71296920 | solution.py:359
  20.8 4.2 convolution_bitcast_fusion
  33.1 13.4 %fusion.29 = bf16[256,768]{1,0:T(8,128)(2,1)S(1)} fusion(f32[256,768]{1,0:T(8,128)S(1)} %get-tuple-element.456, bf16[3072,768]{1,0:T(8,128)(2,1)} %get-tuple-element.208, f32[3072]{0:T(1024)S(1)} %copy-done.88, bf16[768,3072]{1,0:T(8,128)(2,1)} %get-tuple-element.206, f32[256,2304]{1,0:T(8,128)} %convolution_bitcast_fusion, f32[768]{0:T(1024)S(1)} %copy-done.106, ...), kind=kOutput, calls=%fused_computation.36 | convolution fusion | flops 2469789696 | bytes 13780992 | tf_op jit(solution)/shard_map/cond/branch_1_fun/dot_general | solution.py:116
  57.6 47.5 %conditional.8 = (f32[768]{0:T(1024)S(1)}, f32[2304]{0:T(1024)}, f32[3072]{0:T(1024)}, f32[768]{0:T(1024)}, bf16[256,3072]{1,0:T(8,128)(2,1)}, /*index=5*/bf16[2...) conditional(s32[]{:T(128)} %convert_element_type.739, ...), branch_computations={%region_14.30_spmd, %region_30.37_spmd} | conditional | flops 8039338496 | bytes 212989632
  69.6 4.2 convolution_bitcast_fusion.2
  80.9 14.2 %fusion.194 = bf16[256,768]{1,0:T(8,128)(2,1)} fusion(f32[256,768]{1,0:T(8,128)S(1)} %get-tuple-element.470, bf16[3072,768]{1,0:T(8,128)(2,1)} %get-tuple-element.237, f32[3072]{0:T(1024)S(1)} %copy-done.89, bf16[768,3072]{1,0:T(8,128)(2,1)} %get-tuple-element.235, f32[256,2304]{1,0:T(8,128)} %convolution_bitcast_fusion.2, f32[768]{0:T(1024)S(1)} %copy-done.107, ...), kind=kOutput, calls=%fused_computation.285 | convolution fusion | flops 2469789696 | bytes 13780992 | tf_op jit(solution)/shard_map/cond/branch_1_fun/dot_general | solution.py:116
  105.2 68.9 %collective-permute-start.1 = (bf16[256,768]{1,0:T(8,128)(2,1)}, bf16[256,768]{1,0:T(8,128)(2,1)S(1)}, u32[]{:S(2)}, u32[]{:S(2)}) collective-permute-start(bf16[256,768]{1,0:T(8,128)(2,1)} %get-tuple-element.411), channel_id=1, source_target_pairs={{0,16},{16,0},{1,17},{17,1},{2,18},{18,2},{3,19},{19,3},{4,20},{20... | collective-permute-start | bytes 1179656 | tf_op jit(solution)/shard_map/ppermute | solution.py:368
  178.1 4.2 fusion.468
  189.6 2.3 copy.155
  196.1 2.5 subtract_convert_fusion.9
  198.6 4.6 fusion.526
  203.2 2.5 convolution_convert_fusion.25
  208.3 9.5 %multiply_convert_fusion.4 = (bf16[256,3072]{1,0:T(8,128)(2,1)S(1)}, f32[256,3072]{1,0:T(8,128)S(1)}, f32[256,3072]{1,0:T(8,128)S(1)}) fusion(f32[3072]{0:T(1024)S(1)} %copy-done.91, bf16[256,768]{1,0:T(8,128)(2,1)S(1)} %fusion.424, bf16[1,768,3072]{2,1,0:T(8,128)(2,1)S(1)} %bitcast.398), kind=kOutput, calls=%fused_computation.541 | convolution fusion | flops 1259864064 | bytes 12988416 | tf_op jit(solution)/shard_map/dot_general | solution.py:112
  220.9 2.7 convert_reduce_fusion.8
  232.4 3.4 convolution_convert_fusion.22
  237.6 6.0 %fusion.398 = f32[256,12,64]{0,2,1:T(8,128)} fusion(bf16[12,256,256]{1,2,0:T(8,128)(2,1)} %convolution_convert_fusion.19, pred[256,256]{0,1:T(8,128)(4,1)} %get-tuple-element.567, bf16[256,12,32]{0,2,1:T(8,128)(2,1)} %get-tuple-element.563, bf16[256,12,32]{0,2,1:T(8,128)(2,1)} %get-tuple-element.564, f32[12,256,256]{1,2,0:T(8,128)} %get-tuple-element.583, ...), kind=kOutput, calls=%fused_computation.603 | convolution fusion | flops 108924160 | bytes 5976064 | tf_op jit(solution)/shard_map/htu,uhd->thd/dot_general | solution.py:205
  243.6 6.0 %fusion.401 = f32[256,12,64]{0,2,1:T(8,128)} fusion(bf16[12,256,256]{1,2,0:T(8,128)(2,1)} %convolution_convert_fusion.19, pred[256,256]{0,1:T(8,128)(4,1)} %get-tuple-element.567, bf16[256,12,32]{0,2,1:T(8,128)(2,1)} %get-tuple-element.554, bf16[256,12,32]{0,2,1:T(8,128)(2,1)} %get-tuple-element.553, f32[12,256,256]{1,2,0:T(8,128)} %get-tuple-element.583, ...), kind=kOutput, calls=%fused_computation.606 | convolution fusion | flops 108924160 | bytes 5976064 | tf_op jit(solution)/shard_map/htu,thd->uhd/dot_general | solution.py:210
  256.3 4.0 fusion.528
  260.3 7.2 %collective-permute-done.2 = bf16[256,768]{1,0:T(8,128)(2,1)} collective-permute-done((bf16[256,768]{1,0:T(8,128)(2,1)}, bf16[256,768]{1,0:T(8,128)(2,1)}, u32[]{:S(2)}, u32[]{:S(2)}) %collective-permute-start.2) | collective-permute-done | bytes 393248 | tf_op jit(solution)/shard_map/ppermute | solution.py:376
  267.5 91.1 %conditional.7 = (f32[768]{0:T(1024)}, f32[2304]{0:T(1024)}, f32[3072]{0:T(1024)}, f32[768]{0:T(1024)}, bf16[256,3072]{1,0:T(8,128)(2,1)}, /*index=5*/bf16[256,7...) conditional(s32[]{:T(128)} %convert_element_type.739, ...), branch_computations={%region_48.49_spmd, %region_49.65_spmd} | conditional | flops 8038748672 | bytes 200070832 | solution.py:377
  277.9 4.1 convolution_bitcast_fusion.3
  292.6 2.5 subtract_convert_fusion.7
  295.1 4.0 fusion.522
  299.1 3.3 convolution_convert_fusion.13
  304.5 2.9 convert_reduce_fusion.7
  307.4 9.1 %multiply_convert_fusion.2 = (bf16[256,3072]{1,0:T(8,128)(2,1)S(1)}, f32[256,3072]{1,0:T(8,128)S(1)}, f32[256,3072]{1,0:T(8,128)S(1)}) fusion(f32[3072]{0:T(1024)S(1)} %copy-done.90, bf16[256,768]{1,0:T(8,128)(2,1)} %get-tuple-element.646, bf16[768,3072]{1,0:T(8,128)(2,1)S(1)} %bitcast.402), kind=kOutput, calls=%fused_computation.381 | convolution fusion | flops 1259864064 | bytes 12988416 | tf_op jit(solution)/shard_map/cond/branch_1_fun/dot_general | solution.py:112
  316.5 4.1 convert_reduce_fusion.5
  320.6 2.7 fusion.294
  325.6 2.5 fusion.524
  334.2 3.4 convolution_convert_fusion.10
  339.4 6.0 %fusion.297 = f32[256,12,64]{0,2,1:T(8,128)} fusion(bf16[12,256,256]{1,2,0:T(8,128)(2,1)} %convolution_convert_fusion.8, pred[256,256]{0,1:T(8,128)(4,1)} %get-tuple-element.257, bf16[256,12,32]{0,2,1:T(8,128)(2,1)} %get-tuple-element.514, bf16[256,12,32]{0,2,1:T(8,128)(2,1)} %get-tuple-element.513, f32[12,256,256]{1,2,0:T(8,128)} %get-tuple-element.524, ...), kind=kOutput, calls=%fused_computation.420 | convolution fusion | flops 108924160 | bytes 5976064 | tf_op jit(solution)/shard_map/cond/branch_1_fun/htu,uhd->thd/dot_general | solution.py:205
  345.3 6.0 %fusion.300 = f32[256,12,64]{0,2,1:T(8,128)} fusion(bf16[12,256,256]{1,2,0:T(8,128)(2,1)} %convolution_convert_fusion.8, pred[256,256]{0,1:T(8,128)(4,1)} %get-tuple-element.257, bf16[256,12,32]{0,2,1:T(8,128)(2,1)} %get-tuple-element.519, bf16[256,12,32]{0,2,1:T(8,128)(2,1)} %get-tuple-element.520, f32[12,256,256]{1,2,0:T(8,128)} %get-tuple-element.524, ...), kind=kOutput, calls=%fused_computation.423 | convolution fusion | flops 108924160 | bytes 5976064 | tf_op jit(solution)/shard_map/cond/branch_1_fun/htu,thd->uhd/dot_general | solution.py:210
  368.1 8.2 %convolution_convert_fusion.16 = bf16[768,2304]{1,0:T(8,128)(2,1)S(1)} fusion(bf16[256,2304]{0,1:T(8,128)(2,1)S(1)} %copy-done.50, bf16[256,768]{0,1:T(8,128)(2,1)S(1)} %bitcast.404, bf16[256,768]{0,1:T(8,128)(2,1)S(1)} %bitcast.388, bf16[256,768]{0,1:T(8,128)(2,1)S(1)} %bitcast.386, bf16[256,768]{1,0:T(8,128)(2,1)} %get-tuple-element.347, ...), kind=kOutput, calls=%fused_computation.503 | convolution fusion | flops 1824718848 | bytes 6684672 | tf_op jit(solution)/shard_map/td,te->de/dot_general | solution.py:272
  378.5 3.9 convolution_convert_fusion.15
  387.1 4.2 convolution_convert_fusion.14
  391.3 3.9 collective-permute-done.4
  399.8 2.3 maximum_select_fusion
  402.2 2.7 collective-permute-start.6
  408.2 3.4 collective-permute-done.6
  414.8 2.7 fusion.338
  419.1 11.4 %collective-permute-done.8 = bf16[2,2,48,2304]{3,2,0,1:T(8,128)(2,1)S(1)} collective-permute-done((bf16[2,2,48,2304]{3,2,0,1:T(8,128)(2,1)}, bf16[2,2,48,2304]{3,2,0,1:T(8,128)(2,1)S(1)}, u32[]{:S(2)}, u32[]{:S(2)}) %collective-permute-start.8) | collective-permute-done | bytes 884768 | tf_op jit(solution)/shard_map/ppermute | solution.py:293
  435.2 20.7 %collective-permute-done.9 = bf16[2,48,2304]{2,1,0:T(8,128)(2,1)S(1)} collective-permute-done((bf16[2,48,2304]{2,1,0:T(8,128)(2,1)S(1)}, bf16[2,48,2304]{2,1,0:T(8,128)(2,1)S(1)}, u32[]{:S(2)}, u32[]{:S(2)}) %collective-permute-start.9) | collective-permute-done | bytes 442400 | tf_op jit(solution)/shard_map/ppermute | solution.py:293
  456.7 3.2 collective-permute-start.13
  459.9 6.3 %collective-permute-done.10 = bf16[48,2304]{1,0:T(8,128)(2,1)S(1)} collective-permute-done((bf16[48,2304]{1,0:T(8,128)(2,1)S(1)}, bf16[48,2304]{1,0:T(8,128)(2,1)S(1)}, u32[]{:S(2)}, u32[]{:S(2)}) %collective-permute-start.10) | collective-permute-done | bytes 221216 | tf_op jit(solution)/shard_map/ppermute | solution.py:293
  466.9 13.1 %collective-permute-done.16 = bf16[2,2,192,768]{3,2,0,1:T(8,128)(2,1)S(1)} collective-permute-done((bf16[2,2,192,768]{3,2,0,1:T(8,128)(2,1)S(1)}, bf16[2,2,192,768]{3,2,0,1:T(8,128)(2,1)S(1)}, u32[]{:S(2)}, u32[]{:S(2)}) %collective-permute-start.16) | collective-permute-done | bytes 1179680 | tf_op jit(solution)/shard_map/ppermute | solution.py:293
  480.6 2.9 collective-permute-start.14
  483.5 17.3 %collective-permute-done.17 = bf16[2,192,768]{2,1,0:T(8,128)(2,1)S(1)} collective-permute-done((bf16[2,192,768]{2,1,0:T(8,128)(2,1)S(1)}, bf16[2,192,768]{2,1,0:T(8,128)(2,1)S(1)}, u32[]{:S(2)}, u32[]{:S(2)}) %collective-permute-start.17) | collective-permute-done | bytes 589856 | tf_op jit(solution)/shard_map/ppermute | solution.py:293
  502.0 13.3 %collective-permute-done.18 = bf16[192,768]{1,0:T(8,128)(2,1)S(1)} collective-permute-done((bf16[192,768]{1,0:T(8,128)(2,1)S(1)}, bf16[192,768]{1,0:T(8,128)(2,1)S(1)}, u32[]{:S(2)}, u32[]{:S(2)}) %collective-permute-start.18) | collective-permute-done | bytes 294944 | tf_op jit(solution)/shard_map/ppermute | solution.py:293
  (453 shorter events, 178.9 us)
Async XLA Ops:
  2.6 10.8 %copy-start.78 = (s32[256]{0:T(256)}, s32[256]{0:T(256)S(1)}, u32[]{:S(2)}) copy-start(s32[256]{0:T(256)S(1)} %convert_reduce_fusion.12) | copy-start | bytes 3076
  4.6 8.8 %copy-start.71 = (s32[256]{0:T(256)}, s32[256]{0:T(256)S(1)}, u32[]{:S(2)}) copy-start(s32[256]{0:T(256)S(1)} %get-tuple-element.594) | copy-start | bytes 3076
  13.4 11.6 %copy-start.1 = (bf16[768,2304]{1,0:T(8,128)(2,1)S(1)}, bf16[768,2304]{1,0:T(8,128)(2,1)}, u32[]{:S(2)}) copy-start(bf16[768,2304]{1,0:T(8,128)(2,1)} %get-tuple-element.198) | copy-start | bytes 10616836 | tf_op jit(solution)/shard_map/cond
  47.0 10.6 %collective-permute-start = (bf16[256,768]{1,0:T(8,128)(2,1)S(1)}, bf16[256,768]{1,0:T(8,128)(2,1)S(1)}, u32[]{:S(2)}, u32[]{:S(2)}) collective-permute-start(bf16[256,768]{1,0:T(8,128)(2,1)S(1)} %get-tuple-element.654), channel_id=1, source_target_pairs={{0,16},{1,17},{2,18},{3,19},{4,20},{5,21},{6,22},{7,23},{8,24},{9,... | collective-permute-start | bytes 1179656 | tf_op jit(solution)/shard_map/ppermute | solution.py:362
  52.3 5.3 %copy-start.79 = (f32[4,128]{1,0:T(4,128)}, f32[4,128]{1,0:T(4,128)S(1)}, u32[]{:S(2)}) copy-start(f32[4,128]{1,0:T(4,128)S(1)} %broadcast_select_fusion.7) | copy-start | bytes 6148
  61.6 12.2 %copy-start.3 = (bf16[768,2304]{1,0:T(8,128)(2,1)S(1)}, bf16[768,2304]{1,0:T(8,128)(2,1)}, u32[]{:S(2)}) copy-start(bf16[768,2304]{1,0:T(8,128)(2,1)} %get-tuple-element.227) | copy-start | bytes 10616836
  61.6 12.2 %copy-start.9 = (bf16[256,768]{1,0:T(8,128)(2,1)S(1)}, bf16[256,768]{1,0:T(8,128)(2,1)}, u32[]{:S(2)}) copy-start(bf16[256,768]{1,0:T(8,128)(2,1)} %get-tuple-element.225) | copy-start | bytes 1179652
  105.1 80.0 %copy-start.87 = (f32[768]{0:T(1024)}, f32[768]{0:T(1024)S(1)}, u32[]{:S(2)}) copy-start(f32[768]{0:T(1024)S(1)} %get-tuple-element.308) | copy-start | bytes 9220
  105.1 82.4 %copy-start.48 = (bf16[256,2304]{0,1:T(8,128)(2,1)}, bf16[256,2304]{0,1:T(8,128)(2,1)S(1)}, u32[]{:S(2)}) copy-start(bf16[256,2304]{0,1:T(8,128)(2,1)S(1)} %get-tuple-element.319) | copy-start | bytes 3538948
  105.1 81.2 %copy-start = (bf16[1,768,2304]{2,1,0:T(8,128)(2,1)S(1)}, bf16[1,768,2304]{2,1,0:T(8,128)(2,1)}, u32[]{:S(2)}) copy-start(bf16[1,768,2304]{2,1,0:T(8,128)(2,1)} %param.22) | copy-start | bytes 10616836
  105.2 78.3 %collective-permute-start.1 = (bf16[256,768]{1,0:T(8,128)(2,1)}, bf16[256,768]{1,0:T(8,128)(2,1)S(1)}, u32[]{:S(2)}, u32[]{:S(2)}) collective-permute-start(bf16[256,768]{1,0:T(8,128)(2,1)} %get-tuple-element.411), channel_id=1, source_target_pairs={{0,16},{16,0},{1,17},{17,1},{2,18},{18,2},{3,19},{19,3},{4,20},{20... | collective-permute-start | bytes 1179656 | tf_op jit(solution)/shard_map/ppermute | solution.py:368
  176.2 8.9 %copy-start.68 = (f32[768]{0:T(1024)}, f32[768]{0:T(1024)S(1)}, u32[]{:S(2)}) copy-start(f32[768]{0:T(1024)S(1)} %mul.1165) | copy-start | bytes 9220
  203.1 5.1 slice-start.6
  203.2 5.1 slice-start.7
  207.9 9.9 %slice-start = ((s8[4718592]{0:T(1024)(128)(4,1)}), s8[4194304]{0:T(1024)(128)(4,1)S(1)}, s32[]{:S(2)}) async-start(s8[4718592]{0:T(1024)(128)(4,1)} %bitcast.340), calls=%async_computation | async-start | bytes 8388608
  208.2 9.6 %copy-start.51 = (bf16[256,768]{1,0:T(8,128)(2,1)}, bf16[256,768]{1,0:T(8,128)(2,1)S(1)}, u32[]{:S(2)}) copy-start(bf16[256,768]{1,0:T(8,128)(2,1)S(1)} %fusion.424) | copy-start | bytes 1179652
  208.2 9.6 %slice-start.1 = ((s8[4718592]{0:T(1024)(128)(4,1)}), s8[524288]{0:T(1024)(128)(4,1)S(1)}, s32[]{:S(2)}) async-start(s8[4718592]{0:T(1024)(128)(4,1)} %bitcast.340), calls=%async_computation.1 | async-start | bytes 1048576
  208.3 9.6 %copy-start.32 = (bf16[1,512,768]{2,1,0:T(8,128)(2,1)S(1)}, bf16[1,512,768]{2,1,0:T(8,128)(2,1)}, u32[]{:S(2)}) copy-start(bf16[1,512,768]{2,1,0:T(8,128)(2,1)} %param.18) | copy-start | bytes 2359300
  208.3 9.6 %copy-start.35 = (bf16[256,768]{1,0:T(8,128)(2,1)S(1)}, bf16[256,768]{1,0:T(8,128)(2,1)}, u32[]{:S(2)}) copy-start(bf16[256,768]{1,0:T(8,128)(2,1)} %copy-done.34) | copy-start | bytes 1179652
  208.3 9.6 %copy-start.86 = (f32[768]{0:T(1024)S(1)}, f32[768]{0:T(1024)}, u32[]{:S(2)}) copy-start(f32[768]{0:T(1024)} %add.518) | copy-start | bytes 9220
  220.2 7.2 %copy-start.30 = (bf16[256,768]{1,0:T(8,128)(2,1)}, bf16[256,768]{1,0:T(8,128)(2,1)S(1)}, u32[]{:S(2)}) copy-start(bf16[256,768]{1,0:T(8,128)(2,1)S(1)} %get-tuple-element.434) | copy-start | bytes 1179652
  255.0 12.5 %collective-permute-start.2 = (bf16[256,768]{1,0:T(8,128)(2,1)}, bf16[256,768]{1,0:T(8,128)(2,1)}, u32[]{:S(2)}, u32[]{:S(2)}) collective-permute-start(bf16[256,768]{1,0:T(8,128)(2,1)} %add_convert_fusion.13), channel_id=1, source_target_pairs={{16,0},{17,1},{18,2},{19,3},{20,4},{21,5},{22,6},{23,7},{24,8},{25... | collective-permute-start | bytes 1179656 | tf_op jit(solution)/shard_map/ppermute | solution.py:376
  269.1 8.7 %copy-start.72 = (f32[256]{0:T(256)}, f32[256]{0:T(256)S(1)}, u32[]{:S(2)}) copy-start(f32[256]{0:T(256)S(1)} %broadcast_multiply_fusion.7) | copy-start | bytes 3076 | tf_op jit(solution)/shard_map/cond
  270.4 7.4 %copy-start.80 = (f32[256]{0:T(256)}, f32[256]{0:T(256)S(1)}, u32[]{:S(2)}) copy-start(f32[256]{0:T(256)S(1)} %fusion.322) | copy-start | bytes 3076 | tf_op jit(solution)/shard_map/cond
  271.1 6.8 %copy-start.64 = (f32[768]{0:T(1024)}, f32[768]{0:T(1024)S(1)}, u32[]{:S(2)}) copy-start(f32[768]{0:T(1024)S(1)} %convert_element_type.589) | copy-start | bytes 9220 | tf_op jit(solution)/shard_map/cond
  299.1 8.2 %slice-start.10 = ((s8[4718592]{0:T(1024)(128)(4,1)}), s8[4194304]{0:T(1024)(128)(4,1)S(1)}, s32[]{:S(2)}) async-start(s8[4718592]{0:T(1024)(128)(4,1)} %bitcast.401), calls=%async_computation.10 | async-start | bytes 8388608 | tf_op jit(solution)/shard_map/cond
  299.1 8.2 %slice-start.11 = ((s8[4718592]{0:T(1024)(128)(4,1)}), s8[524288]{0:T(1024)(128)(4,1)S(1)}, s32[]{:S(2)}) async-start(s8[4718592]{0:T(1024)(128)(4,1)} %bitcast.401), calls=%async_computation.11 | async-start | bytes 1048576 | tf_op jit(solution)/shard_map/cond
  304.5 12.0 %slice-start.4 = ((s8[4718592]{0:T(1024)(128)(4,1)}), s8[4194304]{0:T(1024)(128)(4,1)S(1)}, s32[]{:S(2)}) async-start(s8[4718592]{0:T(1024)(128)(4,1)} %bitcast.344), calls=%async_computation.4 | async-start | bytes 8388608 | tf_op jit(solution)/shard_map/cond
  307.3 9.1 %slice-start.5 = ((s8[4718592]{0:T(1024)(128)(4,1)}), s8[524288]{0:T(1024)(128)(4,1)S(1)}, s32[]{:S(2)}) async-start(s8[4718592]{0:T(1024)(128)(4,1)} %bitcast.344), calls=%async_computation.5 | async-start | bytes 1048576 | tf_op jit(solution)/shard_map/cond
  316.5 4.1 copy-start.109
  366.6 15.8 %collective-permute-start.3 = (bf16[2,2,2,80,768]{4,3,2,1,0:T(8,128)(2,1)S(1)}, bf16[2,2,2,80,768]{4,3,2,1,0:T(8,128)(2,1)S(1)}, u32[]{:S(2)}, u32[]{:S(2)}) collective-permute-start(bf16[2,2,2,80,768]{4,3,2,1,0:T(8,128)(2,1)S(1)} %dynamic-slice_bitcast_fusion.2), channel_id=1, source_target_pairs={{0,1},{1,0},{2,3},{3,2},{4,5},{5,4},{6,7},{7,6},{8,9},{9,8},{10,11... | collective-permute-start | bytes 2949128 | tf_op jit(solution)/shard_map/ppermute | solution.py:293
  376.7 28.2 %collective-permute-start.7 = (bf16[2,2,2,48,2304]{4,3,0,2,1:T(8,128)(2,1)S(1)}, bf16[2,2,2,48,2304]{4,3,0,2,1:T(8,128)(2,1)S(1)}, u32[]{:S(2)}, u32[]{:S(2)}) collective-permute-start(bf16[2,2,2,48,2304]{4,3,0,2,1:T(8,128)(2,1)S(1)} %bitcast.359), channel_id=1, source_target_pairs={{0,1},{1,0},{2,3},{3,2},{4,5},{5,4},{6,7},{7,6},{8,9},{9,8},{10,11... | collective-permute-start | bytes 5308424 | tf_op jit(solution)/shard_map/ppermute | solution.py:293
  382.8 12.4 %collective-permute-start.4 = (bf16[2,2,80,768]{3,2,1,0:T(8,128)(2,1)S(1)}, bf16[2,2,80,768]{3,2,1,0:T(8,128)(2,1)S(1)}, u32[]{:S(2)}, u32[]{:S(2)}) collective-permute-start(bf16[2,2,80,768]{3,2,1,0:T(8,128)(2,1)S(1)} %dynamic-slice_bitcast_fusion.6), channel_id=1, source_target_pairs={{0,2},{1,3},{2,0},{3,1},{4,6},{5,7},{6,4},{7,5},{8,10},{9,11},{10,... | collective-permute-start | bytes 1474568 | tf_op jit(solution)/shard_map/ppermute | solution.py:293
  385.9 28.9 %collective-permute-start.11 = (bf16[2,2,2,48,3072]{4,3,0,1,2:T(8,128)(2,1)}, bf16[2,2,2,48,3072]{4,3,0,1,2:T(8,128)(2,1)}, u32[]{:S(2)}, u32[]{:S(2)}) collective-permute-start(bf16[2,2,2,48,3072]{4,3,0,1,2:T(8,128)(2,1)} %bitcast.320), channel_id=1, source_target_pairs={{0,1},{1,0},{2,3},{3,2},{4,5},{5,4},{6,7},{7,6},{8,9},{9,8},{10,11... | collective-permute-start | bytes 7077896 | tf_op jit(solution)/shard_map/ppermute | solution.py:293
  395.3 6.8 %collective-permute-start.5 = (bf16[2,80,768]{2,1,0:T(8,128)(2,1)S(1)}, bf16[2,80,768]{2,1,0:T(8,128)(2,1)S(1)}, u32[]{:S(2)}, u32[]{:S(2)}) collective-permute-start(bf16[2,80,768]{2,1,0:T(8,128)(2,1)S(1)} %dynamic-slice_bitcast_fusion.10), channel_id=1, source_target_pairs={{0,4},{1,5},{2,6},{3,7},{4,0},{5,1},{6,2},{7,3},{8,12},{9,13},{10,... | collective-permute-start | bytes 737288 | tf_op jit(solution)/shard_map/ppermute | solution.py:293
  399.8 32.5 %collective-permute-start.15 = (bf16[2,2,2,192,768]{4,3,0,1,2:T(8,128)(2,1)}, bf16[2,2,2,192,768]{4,3,0,1,2:T(8,128)(2,1)}, u32[]{:S(2)}, u32[]{:S(2)}) collective-permute-start(bf16[2,2,2,192,768]{4,3,0,1,2:T(8,128)(2,1)} %bitcast.319), channel_id=1, source_target_pairs={{0,1},{1,0},{2,3},{3,2},{4,5},{5,4},{6,7},{7,6},{8,9},{9,8},{10,11... | collective-permute-start | bytes 7077896 | tf_op jit(solution)/shard_map/ppermute | solution.py:293
  402.2 9.4 %collective-permute-start.6 = (bf16[80,768]{1,0:T(8,128)(2,1)S(1)}, bf16[80,768]{1,0:T(8,128)(2,1)S(1)}, u32[]{:S(2)}, u32[]{:S(2)}) collective-permute-start(bf16[80,768]{1,0:T(8,128)(2,1)S(1)} %dynamic-slice_bitcast_fusion.12), channel_id=1, source_target_pairs={{0,8},{1,9},{2,10},{3,11},{4,12},{5,13},{6,14},{7,15},{8,0},{9,1},... | collective-permute-start | bytes 368648 | tf_op jit(solution)/shard_map/ppermute | solution.py:293
  407.6 22.9 %collective-permute-start.8 = (bf16[2,2,48,2304]{3,2,0,1:T(8,128)(2,1)}, bf16[2,2,48,2304]{3,2,0,1:T(8,128)(2,1)S(1)}, u32[]{:S(2)}, u32[]{:S(2)}) collective-permute-start(bf16[2,2,48,2304]{3,2,0,1:T(8,128)(2,1)} %dynamic-slice_bitcast_fusion.3), channel_id=1, source_target_pairs={{0,4},{1,5},{2,6},{3,7},{4,0},{5,1},{6,2},{7,3},{8,12},{9,13},{10,... | collective-permute-start | bytes 2654216 | tf_op jit(solution)/shard_map/ppermute | solution.py:293
  414.8 15.7 %copy-start.23 = (bf16[2,2,2,48,2304]{4,3,0,2,1:T(8,128)(2,1)S(1)}, bf16[2,2,2,48,2304]{4,3,0,2,1:T(8,128)(2,1)}, u32[]{:S(2)}) copy-start(bf16[2,2,2,48,2304]{4,3,0,2,1:T(8,128)(2,1)} %copy-done.22) | copy-start | bytes 5308420
  417.5 14.8 %copy-start.21 = (bf16[2,2,2,1,192,768]{5,4,3,2,1,0:T(8,128)(2,1)S(1)}, bf16[2,2,2,1,192,768]{5,4,3,2,1,0:T(8,128)(2,1)}, u32[]{:S(2)}) copy-start(bf16[2,2,2,1,192,768]{5,4,3,2,1,0:T(8,128)(2,1)} %get-tuple-element.538) | copy-start | bytes 7077892
  417.6 38.6 %collective-permute-start.12 = (bf16[2,2,48,3072]{3,2,0,1:T(8,128)(2,1)S(1)}, bf16[2,2,48,3072]{3,2,0,1:T(8,128)(2,1)S(1)}, u32[]{:S(2)}, u32[]{:S(2)}) collective-permute-start(bf16[2,2,48,3072]{3,2,0,1:T(8,128)(2,1)S(1)} %dynamic-slice_bitcast_fusion.1), channel_id=1, source_target_pairs={{0,2},{1,3},{2,0},{3,1},{4,6},{5,7},{6,4},{7,5},{8,10},{9,11},{10,... | collective-permute-start | bytes 3538952 | tf_op jit(solution)/shard_map/ppermute | solution.py:293
  430.7 25.2 %collective-permute-start.9 = (bf16[2,48,2304]{2,1,0:T(8,128)(2,1)S(1)}, bf16[2,48,2304]{2,1,0:T(8,128)(2,1)S(1)}, u32[]{:S(2)}, u32[]{:S(2)}) collective-permute-start(bf16[2,48,2304]{2,1,0:T(8,128)(2,1)S(1)} %dynamic-slice_bitcast_fusion.7), channel_id=1, source_target_pairs={{0,2},{1,3},{2,0},{3,1},{4,6},{5,7},{6,4},{7,5},{8,10},{9,11},{10,... | collective-permute-start | bytes 1327112 | tf_op jit(solution)/shard_map/ppermute | solution.py:293
  434.6 45.4 %collective-permute-start.16 = (bf16[2,2,192,768]{3,2,0,1:T(8,128)(2,1)S(1)}, bf16[2,2,192,768]{3,2,0,1:T(8,128)(2,1)S(1)}, u32[]{:S(2)}, u32[]{:S(2)}) collective-permute-start(bf16[2,2,192,768]{3,2,0,1:T(8,128)(2,1)S(1)} %dynamic-slice_bitcast_fusion), channel_id=1, source_target_pairs={{0,2},{1,3},{2,0},{3,1},{4,6},{5,7},{6,4},{7,5},{8,10},{9,11},{10,... | collective-permute-start | bytes 3538952 | tf_op jit(solution)/shard_map/ppermute | solution.py:293
  456.1 10.0 %collective-permute-start.10 = (bf16[48,2304]{1,0:T(8,128)(2,1)S(1)}, bf16[48,2304]{1,0:T(8,128)(2,1)S(1)}, u32[]{:S(2)}, u32[]{:S(2)}) collective-permute-start(bf16[48,2304]{1,0:T(8,128)(2,1)S(1)} %dynamic-slice_bitcast_fusion.11), channel_id=1, source_target_pairs={{0,8},{1,9},{2,10},{3,11},{4,12},{5,13},{6,14},{7,15},{8,0},{9,1},... | collective-permute-start | bytes 663560 | tf_op jit(solution)/shard_map/ppermute | solution.py:293
  456.7 23.7 %collective-permute-start.13 = (bf16[2,48,3072]{2,1,0:T(8,128)(2,1)S(1)}, bf16[2,48,3072]{2,1,0:T(8,128)(2,1)S(1)}, u32[]{:S(2)}, u32[]{:S(2)}) collective-permute-start(bf16[2,48,3072]{2,1,0:T(8,128)(2,1)S(1)} %dynamic-slice_bitcast_fusion.5), channel_id=1, source_target_pairs={{0,4},{1,5},{2,6},{3,7},{4,0},{5,1},{6,2},{7,3},{8,12},{9,13},{10,... | collective-permute-start | bytes 1769480 | tf_op jit(solution)/shard_map/ppermute | solution.py:293
  480.4 20.4 %collective-permute-start.17 = (bf16[2,192,768]{2,1,0:T(8,128)(2,1)S(1)}, bf16[2,192,768]{2,1,0:T(8,128)(2,1)S(1)}, u32[]{:S(2)}, u32[]{:S(2)}) collective-permute-start(bf16[2,192,768]{2,1,0:T(8,128)(2,1)S(1)} %dynamic-slice_bitcast_fusion.4), channel_id=1, source_target_pairs={{0,4},{1,5},{2,6},{3,7},{4,0},{5,1},{6,2},{7,3},{8,12},{9,13},{10,... | collective-permute-start | bytes 1769480 | tf_op jit(solution)/shard_map/ppermute | solution.py:293
  480.6 20.5 %collective-permute-start.14 = (bf16[48,3072]{1,0:T(8,128)(2,1)S(1)}, bf16[48,3072]{1,0:T(8,128)(2,1)S(1)}, u32[]{:S(2)}, u32[]{:S(2)}) collective-permute-start(bf16[48,3072]{1,0:T(8,128)(2,1)S(1)} %dynamic-slice_bitcast_fusion.9), channel_id=1, source_target_pairs={{0,8},{1,9},{2,10},{3,11},{4,12},{5,13},{6,14},{7,15},{8,0},{9,1},... | collective-permute-start | bytes 884744 | tf_op jit(solution)/shard_map/ppermute | solution.py:293
  501.0 14.3 %collective-permute-start.18 = (bf16[192,768]{1,0:T(8,128)(2,1)S(1)}, bf16[192,768]{1,0:T(8,128)(2,1)S(1)}, u32[]{:S(2)}, u32[]{:S(2)}) collective-permute-start(bf16[192,768]{1,0:T(8,128)(2,1)S(1)} %dynamic-slice_bitcast_fusion.8), channel_id=1, source_target_pairs={{0,8},{1,9},{2,10},{3,11},{4,12},{5,13},{6,14},{7,15},{8,0},{9,1},... | collective-permute-start | bytes 884744 | tf_op jit(solution)/shard_map/ppermute | solution.py:293
  (73 other events, 135.6 us)

commit v2 on v1

v2 whole, which is shorter than its diff:
```python
from functools import partial
import math

import jax
import jax.numpy as jnp
from jax import lax
from jax.experimental import pallas as pl
from jax.experimental.pallas import tpu as pltpu
from jax.sharding import PartitionSpec as P

HEADS = 12
HEAD = 64
EMB = 128
SEGS = 4

ANY = pl.ANY
VMEM = pltpu.MemorySpace.VMEM
SMEM = pltpu.MemorySpace.SMEM
F32 = jnp.float32
BF16 = jnp.bfloat16
ROOT_HALF = 0.7071067811865476
ROOT_TAU = 0.3989422804014327


def dot(left, right, left_dim=1, right_dim=0):
    return lax.dot_general(
        left, right, (((left_dim,), (right_dim,)), ((), ())), preferred_element_type=F32
    )


def lane_blocks(values, size=128):
    return [values[:, i : i + size] for i in range(0, values.shape[1], size)]


def swap_halves(values, low_half):
    forth = pltpu.roll(values, 128 - HEAD // 2, 1)
    back = pltpu.roll(values, HEAD // 2, 1)
    return jnp.where(low_half, forth, back)


def norm_parts(values):
    center = values - jnp.mean(values, axis=-1, keepdims=True)
    spread = jnp.mean(center * center, axis=-1, keepdims=True)
    factor = lax.rsqrt(spread + 1e-05)
    return center * factor, factor


def norm_back(grad, unit, factor):
    return factor * (
        grad
        - jnp.mean(grad, axis=-1, keepdims=True)
        - unit * jnp.mean(grad * unit, axis=-1, keepdims=True)
    )


OPERANDS = ("normed", "mixed", "modded", "active", "bgrad", "pgrad", "agrad", "jgrad")


def relay_kernel(span, width, hidden, with_back, carried_count, *refs):
    refs = list(refs)
    flags, local, came, mods, trig, gain, ebias, rbias = refs[:8]
    big_hbm = refs[8:12]
    pos = 12 + carried_count
    leave = refs[pos]
    pos += 1
    if with_back:
        ends, small_out = refs[pos : pos + 2]
        ops_out = dict(zip(OPERANDS, refs[pos + 2 : pos + 2 + len(OPERANDS)]))
        pos += 2 + len(OPERANDS)
    (
        xv, dyv, win, wout, wex, wre, qkv, probs, middle, slope, branch, mixed_grad,
        middle_grad, acc, bias, leave_v, small, *rest,
    ) = refs[pos:]
    ops = dict(zip(OPERANDS, rest[: len(OPERANDS)]))
    result_v, in_sem, out_sem = rest[len(OPERANDS) :]
    mode, slot, first, single = flags[0], flags[1], flags[2], flags[3]
    pairs = width // 128
    seg = span // SEGS
    step = 512
    tiles = hidden // step
    low_half = lax.broadcasted_iota(jnp.int32, (span, 128), 1) % HEAD < HEAD // 2
    low_head = lax.broadcasted_iota(jnp.int32, (span, 128), 1) < HEAD
    head_row = [
        (lax.broadcasted_iota(jnp.int32, (1, 128), 1) // HEAD == i).astype(F32).astype(BF16)
        for i in range(2)
    ]

    def trig_pair():
        cos_all, sin_all = trig[0], trig[1]
        cos_cut = jnp.concatenate([cos_all[:seg]] * SEGS, axis=0)
        sin_cut = jnp.concatenate([sin_all[:seg]] * SEGS, axis=0)
        whole = single == 1
        return jnp.where(whole, cos_all, cos_cut), jnp.where(whole, sin_all, sin_cut)

    def mod_row(block, part):
        row = jnp.where(single == 1, 0, block)
        return mods[slot, pl.ds(row, 1), part * width : (part + 1) * width]

    own = local.at[pl.ds(pl.multiple_of(slot * span, span), span)]
    big = (win, wout, wex, wre)
    loads = [
        pltpu.make_async_copy(source, target, in_sem.at[i])
        for i, (source, target) in enumerate(zip(big_hbm, big))
    ]

    def token_loads():
        mine = first == 1

        @pl.when(mine)
        def _():
            pltpu.make_async_copy(own, xv, in_sem.at[4]).start()

        @pl.when(jnp.logical_not(mine))
        def _():
            pltpu.make_async_copy(came, xv, in_sem.at[4]).start()

        if with_back:

            @pl.when(mine & (mode == 2))
            def _():
                pltpu.make_async_copy(came, dyv, in_sem.at[5]).start()

            @pl.when(jnp.logical_not(mine) & (mode == 2))
            def _():
                pltpu.make_async_copy(own, dyv, in_sem.at[5]).start()

    def forward_part():
        token_loads()
        for load in loads:
            load.start()
        pltpu.make_async_copy(came, xv, in_sem.at[4]).wait()
        unit, _ = norm_parts(xv[...].astype(F32))
        ops["normed"][...] = (unit * gain[...].astype(F32)).astype(BF16)
        across = lax.broadcasted_iota(jnp.int32, (span, span), 0) // seg
        down = lax.broadcasted_iota(jnp.int32, (span, span), 1) // seg
        bias[...] = jnp.where((across == down) | (single == 1), 0.0, -1e30)
        loads[0].wait()

        def turned(tile, factor):
            cos_part, sin_part = trig_pair()

            def body(i, _):
                at = pl.ds(pl.multiple_of(tile * width + i * 256, 256), 256)
                joint = dot(ops["normed"][...], win[:, at])
                outs = []
                for piece in lane_blocks(joint):
                    outs.append(piece * cos_part + swap_halves(piece, low_half) * sin_part)
                whole = jnp.concatenate(outs, axis=1)
                qkv[:, at] = (whole * factor if factor != 1.0 else whole).astype(BF16)
                return _

            lax.fori_loop(0, width // 256, body, 0)

        turned(0, 0.125)
        turned(1, 1.0)
        qkv[:, 2 * width :] = dot(ops["normed"][...], win[:, 2 * width :]).astype(BF16)

        def heads(i, _):
            at = [pl.ds(pl.multiple_of(p * width + i * 128, 128), 128) for p in range(3)]
            query, key, value = (qkv[:, a] for a in at)
            outs = []
            for h in range(2):
                scores = dot(key * head_row[h], query, 1, 1) + bias[...]
                top = jnp.max(scores, axis=0, keepdims=True)
                raised = jnp.exp(scores - top)
                total = jnp.sum(raised, axis=0, keepdims=True)
                prob = raised * (1.0 / total)
                probs[2 * i + h] = prob
                outs.append(dot(prob.astype(BF16), value, 0, 0))
            ops["mixed"][:, at[0]] = jnp.where(low_head, outs[0], outs[1]).astype(BF16)
            return _

        lax.fori_loop(0, pairs, heads, 0)
        loads[1].wait()
        middle[...] = xv[...].astype(F32) + dot(ops["mixed"][...], wout[...])
        for b in range(SEGS):
            rows = slice(b * seg, (b + 1) * seg)
            unit, _ = norm_parts(middle[rows])
            ops["modded"][rows] = (unit * (1.0 + mod_row(b, 0)) + mod_row(b, 1)).astype(BF16)
        loads[2].wait()
        loads[3].wait()
        branch[...] = jnp.broadcast_to(rbias[...].astype(F32), (span, width))

        def feed(j, _):
            at = pl.ds(pl.multiple_of(j * step, step), step)
            pre = dot(ops["modded"][...], wex[:, at]) + ebias[:, at].astype(F32)
            area = 0.5 + 0.5 * lax.erf(pre * ROOT_HALF)
            active = (pre * area).astype(BF16)
            if with_back:
                slope[:, at] = area + pre * (jnp.exp(pre * pre * -0.5) * ROOT_TAU)
            ops["active"][:, at] = active
            branch[...] += dot(active, wre[at, :])
            return _

        lax.fori_loop(0, tiles, feed, 0)
        for b in range(SEGS):
            rows = slice(b * seg, (b + 1) * seg)
            result = (middle[rows] + mod_row(b, 2) * branch[rows]).astype(BF16)
            result_v[rows] = result

    def send_out(name, index):
        return pltpu.make_async_copy(ops[name], ops_out[name], out_sem.at[index])

    def backward_part():
        outs = {name: send_out(name, i) for i, name in enumerate(OPERANDS)}
        for name in ("normed", "mixed", "modded", "active"):
            outs[name].start()
        pltpu.make_async_copy(came, dyv, in_sem.at[5]).wait()
        small[...] = jnp.zeros(small.shape, F32)
        whole = single == 1

        def add_segment(block, part, sums):
            row = jnp.where(whole, 0, block)
            at = (pl.ds(SEGS + row, 1), slice(part * width, (part + 1) * width))
            small[at] = small[at] + sums

        total = jnp.zeros((1, width), F32)
        for b in range(SEGS):
            rows = slice(b * seg, (b + 1) * seg)
            cotan = dyv[rows].astype(F32)
            grad = (cotan * mod_row(b, 2)).astype(BF16)
            ops["bgrad"][rows] = grad
            total += jnp.sum(grad.astype(F32), axis=0, keepdims=True)
            add_segment(b, 2, jnp.sum(cotan * branch[rows], axis=0, keepdims=True))
        small[1:2, width : 2 * width] = total
        outs["bgrad"].start()
        acc[...] = jnp.zeros(acc.shape, F32)

        def feed(j, _):
            at = pl.ds(pl.multiple_of(j * step, step), step)
            grad = dot(ops["bgrad"][...], wre[at, :], 1, 1).astype(BF16).astype(F32)
            pre_grad = (slope[:, at] * grad).astype(BF16)
            ops["pgrad"][:, at] = pre_grad
            small[0:1, at] = jnp.sum(pre_grad.astype(F32), axis=0, keepdims=True)
            acc[...] += dot(pre_grad, wex[:, at], 1, 1)
            return _

        lax.fori_loop(0, tiles, feed, 0)
        outs["pgrad"].start()
        for b in range(SEGS):
            rows = slice(b * seg, (b + 1) * seg)
            grad = acc[rows].astype(BF16).astype(F32)
            unit, factor = norm_parts(middle[rows])
            add_segment(b, 0, jnp.sum(grad * unit, axis=0, keepdims=True))
            add_segment(b, 1, jnp.sum(grad, axis=0, keepdims=True))
            back = norm_back(grad * (1.0 + mod_row(b, 0)), unit, factor)
            full = dyv[rows].astype(F32) + back
            middle_grad[rows] = full
            ops["agrad"][rows] = full.astype(BF16)
        outs["agrad"].start()
        mixed_grad[...] = dot(ops["agrad"][...], wout[...], 1, 1).astype(BF16)
        cos_part, sin_part = trig_pair()

        def heads(i, _):
            at = [pl.ds(pl.multiple_of(p * width + i * 128, 128), 128) for p in range(3)]
            query, key, value = (qkv[:, a] for a in at)
            out_grad = mixed_grad[:, at[0]]
            parts = []
            for h in range(2):
                prob = probs[2 * i + h]
                pull = dot(value * head_row[h], out_grad, 1, 1).astype(BF16).astype(F32)
                shared = jnp.sum(prob * pull, axis=0, keepdims=True)
                score_grad = (prob * (pull - shared)).astype(BF16)
                parts.append(
                    (
                        dot(score_grad, key, 0, 0),
                        dot(score_grad, query),
                        dot(prob.astype(BF16), out_grad),
                    )
                )
            for p in range(3):
                grad = jnp.where(low_head, parts[0][p], parts[1][p])
                if p < 2:
                    grad = grad.astype(BF16).astype(F32)
                    grad = grad * cos_part - swap_halves(grad, low_half) * sin_part
                    if p == 0:
                        grad = grad * 0.125
                ops["jgrad"][:, at[p]] = grad.astype(BF16)
            return _

        lax.fori_loop(0, pairs, heads, 0)
        outs["jgrad"].start()
        acc[...] = dot(ops["jgrad"][...], win[...], 1, 1)
        total = jnp.zeros((1, width), F32)
        for b in range(SEGS):
            rows = slice(b * seg, (b + 1) * seg)
            grad = acc[rows].astype(BF16).astype(F32)
            unit, factor = norm_parts(xv[rows].astype(F32))
            total += jnp.sum(grad * unit, axis=0, keepdims=True)
            back = norm_back(grad * gain[...].astype(F32), unit, factor)
            leave_v[rows] = (middle_grad[rows] + back).astype(BF16)
        small[1:2, 0:width] = total
        end_rows = ends.at[pl.ds(pl.multiple_of(slot * span, span), span)]
        mine = first == 1

        @pl.when(mine)
        def _():
            pltpu.make_async_copy(leave_v, end_rows, out_sem.at[8]).start()

        @pl.when(jnp.logical_not(mine))
        def _():
            pltpu.make_async_copy(result_v, end_rows, out_sem.at[8]).start()

        away = pltpu.make_async_copy(leave_v, leave, out_sem.at[9])
        away.start()
        rest_out = pltpu.make_async_copy(small, small_out, out_sem.at[10])
        rest_out.start()
        for name in OPERANDS:
            outs[name].wait()
        pltpu.make_async_copy(leave_v, end_rows, out_sem.at[8]).wait()
        away.wait()
        rest_out.wait()

    @pl.when(mode >= 1)
    def _():
        forward_part()

    @pl.when(mode == 1)
    def _():
        away = pltpu.make_async_copy(result_v, leave, out_sem.at[9])
        away.start()
        away.wait()

    if with_back:

        @pl.when(mode == 2)
        def _():
            backward_part()


def relay_call(flags, local, came, mods, trig, rows, big, carried, with_back):
    span = came.shape[0]
    width = came.shape[1]
    hidden = big[2].shape[1]
    shapes = {
        "normed": width,
        "mixed": width,
        "modded": width,
        "active": hidden,
        "bgrad": width,
        "pgrad": hidden,
        "agrad": width,
        "jgrad": 3 * width,
    }
    tok = lambda cols, kind=BF16: jax.ShapeDtypeStruct((span, cols), kind)
    outs = [tok(width)]
    if with_back:
        outs += [
            jax.ShapeDtypeStruct(local.shape, BF16),
            jax.ShapeDtypeStruct((2 * SEGS, hidden), F32),
        ]
        outs += [tok(shapes[name]) for name in OPERANDS]
    in_specs = [pl.BlockSpec(memory_space=SMEM), pl.BlockSpec(memory_space=ANY)]
    in_specs += [pl.BlockSpec(memory_space=ANY)]
    in_specs += [pl.BlockSpec(memory_space=VMEM)] * 5
    in_specs += [pl.BlockSpec(memory_space=ANY)] * 4
    args = [flags, local, came, mods, trig, *rows, *big]
    aliases = {}
    for i, item in enumerate(carried):
        aliases[len(args)] = 1 + i
        args.append(item)
        in_specs.append(pl.BlockSpec(memory_space=ANY))
    scratch = lambda cols, kind=BF16: pltpu.VMEM((span, cols), kind)
    scratch_shapes = [
        scratch(width),
        scratch(width),
        *[pltpu.VMEM(item.shape, BF16) for item in big],
        scratch(3 * width),
        pltpu.VMEM((HEADS, span, span), F32),
        scratch(width, F32),
        scratch(hidden, F32),
        scratch(width, F32),
        scratch(width),
        scratch(width, F32),
        scratch(width, F32),
        scratch(span, F32),
        scratch(width),
        pltpu.VMEM((2 * SEGS, hidden), F32),
        *[scratch(shapes[name]) for name in OPERANDS],
        scratch(width),
        pltpu.SemaphoreType.DMA((6,)),
        pltpu.SemaphoreType.DMA((11,)),
    ]
    return pl.pallas_call(
        partial(relay_kernel, span, width, hidden, with_back, len(carried)),
        out_shape=outs,
        in_specs=in_specs,
        out_specs=[pl.BlockSpec(memory_space=ANY)] * len(outs),
        input_output_aliases=aliases,
        scratch_shapes=scratch_shapes,
        compiler_params=pltpu.CompilerParams(
            vmem_limit_bytes=56 * 1024 * 1024
        ),
        name="relay_both" if with_back else "relay_forward",
    )(*args)


def term_kernel(lines, core, left_x, left_y, right_x, right_y, send, keep):
    term = dot(left_x[...], right_x[...], 0, 0) + dot(left_y[...], right_y[...], 0, 0)
    low = core[0] == 0
    for p in range(send.shape[0]):
        even = term[2 * p * lines : (2 * p + 1) * lines]
        odd = term[(2 * p + 1) * lines : (2 * p + 2) * lines]
        send[p] = jnp.where(low, odd, even).astype(BF16)
        keep[p] = jnp.where(low, even, odd)


def weight_term(core, left, right, count, name):
    span, rows = left[0].shape
    cols = right[0].shape[1]
    lines = rows // count
    high, wide = 384, 768
    if lines % 16 or high % (2 * lines):
        term = dot(left[0], right[0], 0, 0) + dot(left[1], right[1], 0, 0)
        view = term.reshape(count // 2, 2, lines, cols)
        own = lax.dynamic_index_in_dim(view, core, 1, keepdims=False)
        other = lax.dynamic_index_in_dim(view, 1 - core, 1, keepdims=False)
        return other.astype(BF16), own
    group = high // (2 * lines)
    left_spec = pl.BlockSpec((span, high), lambda i, j: (0, i))
    right_spec = pl.BlockSpec((span, wide), lambda i, j: (0, j))
    out_spec = pl.BlockSpec((group, lines, wide), lambda i, j: (i, 0, j))
    shape = (count // 2, lines, cols)
    return pl.pallas_call(
        partial(term_kernel, lines),
        grid=(rows // high, cols // wide),
        out_shape=[jax.ShapeDtypeStruct(shape, BF16), jax.ShapeDtypeStruct(shape, F32)],
        in_specs=[
            pl.BlockSpec(memory_space=SMEM),
            left_spec,
            left_spec,
            right_spec,
            right_spec,
        ],
        out_specs=[out_spec, out_spec],
        cost_estimate=pl.CostEstimate(
            flops=4 * span * rows * cols, bytes_accessed=6 * rows * cols, transcendentals=0
        ),
        compiler_params=pltpu.CompilerParams(vmem_limit_bytes=32 * 1024 * 1024),
        name=name,
    )(core.reshape(1), left[0], left[1], right[0], right[1])


def bits_of(count):
    bits = count.bit_length() - 1
    assert 1 << bits == count
    return bits


def halve_sum(send, keep, axis, order):
    count = 2 * keep.shape[0]
    bits = bits_of(count)
    me = lax.axis_index(axis)
    left = list(range(bits - 1, 0, -1))
    terms = [keep.reshape((2,) * (bits - 1) + keep.shape[1:])]
    for step, bit in enumerate(order):
        route = [(i, i ^ (1 << bit)) for i in range(count)]
        if step:
            spot = left.index(bit)
            own = (me >> bit) & 1
            cut = lambda item, at: lax.dynamic_index_in_dim(item, at, spot, keepdims=False)
            send = sum(cut(term, 1 - own).astype(F32) for term in terms).astype(BF16)
            terms = [cut(term, own) for term in terms]
            left.remove(bit)
        came = lax.ppermute(send, axis, route)
        terms.append(came.reshape((2,) * len(left) + keep.shape[1:]))
    return sum(term.astype(F32) for term in terms)


def per_device(
    ends_in,
    lengths,
    times,
    norm_gain,
    attend_in,
    attend_out,
    time_weight,
    time_bias,
    expand_weight,
    expand_bias,
    reduce_weight,
    reduce_bias,
):
    local = ends_in[0]
    micro = lengths.shape[1]
    assert micro == 2
    width = local.shape[1]
    span = local.shape[0] // micro
    hidden = expand_weight.shape[2]
    count = lax.axis_size("rep")
    section = lax.axis_index("section")
    core = lax.axis_index("rep") & 1
    first = 1 - section
    half = HEAD // 2
    freqs = jnp.exp(-math.log(10000.0) * jnp.arange(half, dtype=F32) / half)
    phase = jnp.arange(span, dtype=F32)[:, None] * freqs[None, :]
    cos_part, sin_part = jnp.cos(phase), jnp.sin(phase)
    trig = jnp.stack(
        [
            jnp.concatenate([cos_part] * 4, axis=1),
            jnp.concatenate([-sin_part, sin_part] * 2, axis=1),
        ]
    )
    steps = jnp.exp(-math.log(10000.0) * jnp.arange(EMB // 2, dtype=F32) / (EMB // 2))
    turn = times[0].astype(F32)[:, :, None] * steps
    embed = jnp.concatenate([jnp.cos(turn), jnp.sin(turn)], axis=2)
    mods = jnp.dot(
        embed.reshape(micro * SEGS, EMB),
        time_weight[0].astype(F32),
        precision=lax.Precision.HIGHEST,
    ) + time_bias.astype(F32)
    mods = mods.reshape(micro, SEGS, 3 * width)
    single = (lengths[0, :, 0] == span).astype(jnp.int32)
    rows = (norm_gain, expand_bias, reduce_bias)
    big = (attend_in[0], attend_out[0], expand_weight[0], reduce_weight[0])

    def phase_call(mode, slot, came, carried, with_back=True):
        flags = jnp.stack([mode, slot, first, single[slot]]).astype(jnp.int32)
        return relay_call(flags, local, came, mods, trig, rows, big, carried, with_back)

    zero = jnp.int32(0)
    (out_a,) = phase_call(first, zero, local[:span], (), False)
    came_a = lax.ppermute(out_a, "section", [(0, 1)])
    out_b, ends, *held_y = phase_call(1 + section, first, came_a, ())
    came_b = lax.ppermute(out_b, "section", [(0, 1), (1, 0)])
    out_c, ends, *held_x = phase_call(zero + 2, section, came_b, (ends,))
    came_c = lax.ppermute(out_c, "section", [(1, 0)])
    _, ends, *held_y = phase_call(2 * first, zero + 1, came_c, (ends, *held_y))
    small_x, *ops_x = held_x
    small_y, *ops_y = held_y
    ops = {name: (a, b) for name, a, b in zip(OPERANDS, ops_x, ops_y)}
    bits = bits_of(count)
    plain = list(range(bits))
    turned = plain if bits < 3 else [0, 2, 1] + plain[3:]

    def share(left, right, name, order):
        send, keep = weight_term(core, ops[left], ops[right], count, name)
        return halve_sum(send, keep, "rep", order)

    share_r = share("active", "bgrad", "term_reduce", plain)
    share_e = share("modded", "pgrad", "term_expand", plain)
    share_i = share("normed", "jgrad", "term_attend_in", turned)
    share_o = share("mixed", "agrad", "term_attend_out", plain)
    seq = jnp.concatenate([small_x[SEGS:, : 3 * width], small_y[SEGS:, : 3 * width]])
    swapped = jnp.where(first == 1, embed, embed[::-1]).reshape(micro * SEGS, EMB)
    grad_t = lax.dot_general(
        swapped, seq, (((0,), (0,)), ((), ())), precision=lax.Precision.HIGHEST
    )
    small = small_x + small_y
    pieces = [
        small[1, :width],
        jnp.sum(small[SEGS:, : 3 * width], axis=0),
        small[0],
        small[1, width : 2 * width],
    ]
    line = jnp.concatenate([piece.reshape(count, -1) for piece in pieces], 1)
    cuts = [piece.shape[0] // count for piece in pieces]
    deep = EMB // count
    line = jnp.pad(line, ((0, 0), (0, -line.shape[1] % 128)))
    flat = jnp.pad(line[:, None], ((0, 0), (0, deep - 1), (0, 0)))
    tail = jnp.concatenate([grad_t.reshape(count, deep, 3 * width), flat], axis=2)
    tail = tail.reshape((count // 2, 2) + tail.shape[1:])
    share_t = halve_sum(
        lax.dynamic_index_in_dim(tail, 1 - core, 1, keepdims=False).astype(BF16),
        lax.dynamic_index_in_dim(tail, core, 1, keepdims=False),
        "rep",
        plain,
    )
    share_w = share_t[:, : 3 * width]
    share_s = share_t[0, 3 * width :]
    spots = [sum(cuts[:i]) for i in range(5)]
    share_gain, share_tb, share_eb, share_rb = (share_s[spots[i] : spots[i + 1]] for i in range(4))
    results = (
        share_gain,
        share_i,
        share_o,
        share_w,
        share_tb,
        share_e,
        share_eb,
        share_r,
        share_rb,
    )
    return (ends[None],) + tuple(piece[None] for piece in results)


def solution(mesh):
    return jax.shard_map(
        per_device,
        mesh=mesh,
        in_specs=(
            P("section", "rep", None),
            P("rep", None, None),
            P("rep", None, None),
            P("section", None),
            P("section", None, None),
            P("section", None, None),
            P("section", None, None),
            P("section", None),
            P("section", None, None),
            P("section", None),
            P("section", None, None),
            P("section", None),
        ),
        out_specs=(
            P("section", "rep", None),
            P("section", "rep"),
            P("section", "rep", None),
            P("section", "rep", None),
            P("section", "rep", None),
            P("section", "rep"),
            P("section", "rep", None),
            P("section", "rep"),
            P("section", "rep", None),
            P("section", "rep"),
        ),
        check_vma=False,
    )
```

time: 518 us -> 314 us (0.61)
  matrix products: 179 us -> 1.47 us
  Pallas kernels: 0 us -> 115 us
  other arithmetic: 86.3 us -> 33.3 us
  starting transfers between devices: 87.3 us -> 44.9 us
  local copies, waits for them, and re-layouts: 56.6 us -> 21.2 us
  loops' own time: 5.88 us -> 0 us
    dot_general x51 -> x2, matrix products: 170 us -> 1.47 us  [the longest x1 1.06 us: per_device(): lax.dot_general(swapped, seq, (((0,), (0,)), ((), ())), precision=lax.Pre...]
    pallas_call x0 -> x8, Pallas kernels: none -> 115 us  [the longest x4 97.9 us: relay_call(): pl.pallas_call(partial(relay_kernel, span, width, hidden, with_back, len(...]
    ppermute x19 -> x23, starting transfers between devices: 87.3 us -> 44.9 us  [the longest x20 26.6 us: halve_sum(): came = lax.ppermute(send, axis, route)]
    reduce_sum x21 -> x1, other arithmetic: 18.1 us -> 0.03 us  [per_device(): jnp.sum(small[SEGS:, :3 * width], axis=0)]
    slice x17 -> x8, local copies, waits for them, and re-layouts: 14.8 us -> 5.39 us  [the longest x3 1.78 us: per_device(): share_s[spots[i]:spots[i + 1]]]
    convert_element_type x36 -> x17, other arithmetic: 26.3 us -> 17.3 us  [the longest x15 15.9 us: halve_sum(): send = sum((cut(term, 1 - own).astype(F32) for term in terms)).astype(BF16)]
    sub x2 -> x0, matrix products: 8.55 us -> none  [forward(): probs = jax.nn.softmax(scores, axis=-1)]
    another operation x11 -> x3, local copies, waits for them, and re-layouts: 8.57 us -> 0.22 us  [per_device(): line = jnp.concatenate([piece.reshape(count, -1) for piece in pieces], 1)]
  transfers between devices with their start and end apart: 19 -> 23, of which waited for: 11 -> 14; matrix products, arithmetic and copies ran while one was open for 11% -> 10% of each run, Pallas kernels for 0% -> 4%
where the time goes in v2:
time: 314 us; the launch traced here: 313 us
  Pallas kernels  115 us (37%)
  waiting for transfers between devices  95.9 us (31%)
  starting transfers between devices  44.9 us (14%)
  other arithmetic  33.3 us (11%)
  local copies, waits for them, and re-layouts  21.2 us (7%)
    pallas_call x4, Pallas kernels, relay_call(): pl.pallas_call(partial(relay_kernel, span, width, hidden, with_back, len(...  97.9 us
    ppermute x20, waiting for transfers between devices, halve_sum(): came = lax.ppermute(send, axis, route)  70.7 us
    ppermute x20, starting transfers between devices, halve_sum(): came = lax.ppermute(send, axis, route)  26.6 us
    pallas_call x4, Pallas kernels, weight_term(): pl.pallas_call(partial(term_kernel, lines), grid=(rows // high, cols // w...  17.5 us
    convert_element_type x15, other arithmetic, halve_sum(): send = sum((cut(term, 1 - own).astype(F32) for term in terms)).astype(BF16)  15.9 us
    ppermute x1, starting transfers between devices, per_device(): came_b = lax.ppermute(out_b, 'section', [(0, 1), (1, 0)])  15.7 us
    unnamed x64, local copies, waits for them, and re-layouts  13.4 us
    ppermute x1, waiting for transfers between devices, per_device(): came_c = lax.ppermute(out_c, 'section', [(1, 0)])  8.91 us
  transfers between devices with their start and end apart: 23, of which 14 were waited for; matrix products, arithmetic and copies ran while one was open for 10% of the time, Pallas kernels for 4%

profile of v2, /device:TPU:0, one launch (start us, length us, event | category | flops | bytes accessed | tf_op | source)
XLA Modules:
  0.0 313.4 jit_solution(11364986000416282846)
XLA Ops:
  4.6 1.8 slice_bitcast_fusion.refs_2_
  7.9 1.2 pad_add_fusion.3.refs_0_
  9.2 17.5 %relay_forward.1 = bf16[256,768]{1,0:T(8,128)(2,1)} custom-call(s32[4]{0:T(128)} %pad_add_fusion.3.refs_0_, bf16[512,768]{1,0:T(8,128)(2,1)} %bitcast.219, bf16[256,768]{1,0:T(8,128)(2,1)} %slice_bitcast_fusion.refs_2_, f32[2,4,2304]{2,1,0:T(4,128)} %reshape.308.refs_3_, f32[2,256,128]{2,1,0:T(8,128)} %pad_maximum_fusion.refs_4_, bf16[1,768]{1,0:T(2,128)(2,1)} %refs_5_.7, ...), custom_call_target="tpu_custom_call" | custom-call | tf_op jit(solution)/shard_map/relay_forward/pallas_call | solution.py:384
  26.7 1.3 collective-permute-start
  28.0 1.3 pad_add_fusion.2.refs_0_
  29.2 8.3 %collective-permute-done.refs_2_ = bf16[256,768]{1,0:T(8,128)(2,1)S(1)} collective-permute-done((bf16[256,768]{1,0:T(8,128)(2,1)}, bf16[256,768]{1,0:T(8,128)(2,1)S(1)}, u32[]{:S(2)}, u32[]{:S(2)}) %collective-permute-start) | collective-permute-done | bytes 393248 | tf_op jit(solution)/shard_map/ppermute | solution.py:523
  38.3 17.8 %relay_both.3 = (bf16[256,768]{1,0:T(8,128)(2,1)}, bf16[512,768]{1,0:T(8,128)(2,1)}, f32[8,3072]{1,0:T(8,128)}, bf16[256,768]{1,0:T(8,128)(2,1)}, bf16[256,768]{...) custom-call(s32[4]{0:T(128)} %pad_add_fusion.2.refs_0_, ...), custom_call_target="tpu_custom_call" | custom-call | tf_op jit(solution)/shard_map/relay_both/pallas_call | solution.py:384
  56.1 15.7 %collective-permute-start.1 = (bf16[256,768]{1,0:T(8,128)(2,1)}, bf16[256,768]{1,0:T(8,128)(2,1)S(1)}, u32[]{:S(2)}, u32[]{:S(2)}) collective-permute-start(bf16[256,768]{1,0:T(8,128)(2,1)} %get-tuple-element.50), channel_id=1, source_target_pairs={{0,16},{16,0},{1,17},{17,1},{2,18},{18,2},{3,19},{19,3},{4,20},{20... | collective-permute-start | bytes 1179656 | tf_op jit(solution)/shard_map/ppermute | solution.py:525
  71.8 1.2 pad_add_fusion.1.refs_0_
  73.1 8.0 %collective-permute-done.1.refs_2_ = bf16[256,768]{1,0:T(8,128)(2,1)S(1)} collective-permute-done((bf16[256,768]{1,0:T(8,128)(2,1)}, bf16[256,768]{1,0:T(8,128)(2,1)S(1)}, u32[]{:S(2)}, u32[]{:S(2)}) %collective-permute-start.1) | collective-permute-done | bytes 393248 | tf_op jit(solution)/shard_map/ppermute | solution.py:525
  81.9 31.2 %relay_both.4 = (bf16[256,768]{1,0:T(8,128)(2,1)}, bf16[512,768]{1,0:T(8,128)(2,1)}, f32[8,3072]{1,0:T(8,128)}, bf16[256,768]{1,0:T(8,128)(2,1)}, bf16[256,768]{...) custom-call(s32[4]{0:T(128)} %pad_add_fusion.1.refs_0_, ...), custom_call_target="tpu_custom_call", output_to_operand_aliasing={{1}: (12, {})} | custom-call | tf_op jit(solution)/shard_map/relay_both/pallas_call | solution.py:384
  113.2 1.3 collective-permute-start.2
  116.7 8.9 %collective-permute-done.2.refs_2_ = bf16[256,768]{1,0:T(8,128)(2,1)S(1)} collective-permute-done((bf16[256,768]{1,0:T(8,128)(2,1)}, bf16[256,768]{1,0:T(8,128)(2,1)S(1)}, u32[]{:S(2)}, u32[]{:S(2)}) %collective-permute-start.2) | collective-permute-done | bytes 393248 | tf_op jit(solution)/shard_map/ppermute | solution.py:527
  126.4 31.4 %relay_both.5 = (bf16[256,768]{1,0:T(8,128)(2,1)}, bf16[512,768]{1,0:T(8,128)(2,1)}, f32[8,3072]{1,0:T(8,128)}, bf16[256,768]{1,0:T(8,128)(2,1)}, bf16[256,768]{...) custom-call(s32[4]{0:T(128)} %pad_add_fusion.refs_0_, ...), custom_call_target="tpu_custom_call", output_to_operand_aliasing={{1}: (12, {}), {2}: (13, {}), {3}: (14, {}), {4}: (15, {}),... | custom-call | tf_op jit(solution)/shard_map/relay_both/pallas_call | solution.py:384
  159.7 1.4 copy-done.6
  162.1 5.6 %term_reduce.1 = (bf16[8,192,768]{2,1,0:T(8,128)(2,1)}, f32[8,192,768]{2,1,0:T(8,128)S(1)}) custom-call(s32[1]{0:T(128)} %bitcast.36.core, bf16[256,3072]{1,0:T(8,128)(2,1)S(1)} %copy-done.15, bf16[256,3072]{1,0:T(8,128)(2,1)S(1)} %copy-done.6, bf16[256,768]{1,0:T(8,128)(2,1)S(1)} %copy-done.21, bf16[256,768]{1,0:T(8,128)(2,1)S(1)} %copy-done.12), custom_call_target="tpu_custom_call" | custom-call | flops 2415919104 | bytes 14155776 | tf_op jit(solution)/shard_map/term_reduce/pallas_call | solution.py:424
  167.8 2.2 copy-done.2
  170.0 6.1 %term_expand.1 = (bf16[8,48,3072]{2,1,0:T(8,128)(2,1)}, f32[8,48,3072]{2,1,0:T(8,128)S(1)}) custom-call(s32[1]{0:T(128)} %bitcast.36.core, bf16[256,768]{1,0:T(8,128)(2,1)S(1)} %copy-done.20, bf16[256,768]{1,0:T(8,128)(2,1)S(1)} %copy-done.11, bf16[256,3072]{1,0:T(8,128)(2,1)S(1)} %copy-done.14, bf16[256,3072]{1,0:T(8,128)(2,1)S(1)} %copy-done.7), custom_call_target="tpu_custom_call" | custom-call | flops 2415919104 | bytes 14155776 | tf_op jit(solution)/shard_map/term_expand/pallas_call | solution.py:424
  176.1 2.2 copy-done.3
  182.1 4.7 %term_attend_in.1 = (bf16[8,48,2304]{2,1,0:T(8,128)(2,1)}, f32[8,48,2304]{2,1,0:T(8,128)S(1)}) custom-call(s32[1]{0:T(128)} %bitcast.36.core, bf16[256,768]{1,0:T(8,128)(2,1)S(1)} %copy-done.19, bf16[256,768]{1,0:T(8,128)(2,1)S(1)} %copy-done.9, bf16[256,2304]{1,0:T(8,128)(2,1)S(1)} %copy-done.16, bf16[256,2304]{1,0:T(8,128)(2,1)S(1)} %copy-done.8), custom_call_target="tpu_custom_call" | custom-call | flops 1811939328 | bytes 10616832 | tf_op jit(solution)/shard_map/term_attend_in/pallas_call | solution.py:424
  186.7 1.9 copy-done.4
  192.9 4.7 %collective-permute-done.4 = bf16[2,2,8,2816]{3,2,1,0:T(8,128)(2,1)} collective-permute-done((bf16[2,2,8,2816]{3,2,1,0:T(8,128)(2,1)}, bf16[2,2,8,2816]{3,2,1,0:T(8,128)(2,1)}, u32[]{:S(2)}, u32[]{:S(2)}) %collective-permute-start.4) | collective-permute-done | bytes 180256 | tf_op jit(solution)/shard_map/ppermute | solution.py:465
  198.7 1.2 collective-permute-start.5
  199.9 3.4 %collective-permute-done.5 = bf16[2,8,2816]{2,1,0:T(8,128)(2,1)S(1)} collective-permute-done((bf16[2,8,2816]{2,1,0:T(8,128)(2,1)S(1)}, bf16[2,8,2816]{2,1,0:T(8,128)(2,1)S(1)}, u32[]{:S(2)}, u32[]{:S(2)}) %collective-permute-start.5) | collective-permute-done | bytes 90144 | tf_op jit(solution)/shard_map/ppermute | solution.py:465
  204.2 2.2 collective-permute-start.6
  206.5 1.5 collective-permute-start.12
  210.2 1.9 fusion.4
  212.1 1.2 collective-permute-start.8
  213.3 2.4 fusion.1
  215.7 1.7 collective-permute-start.20
  217.4 1.7 fusion
  223.1 11.2 %collective-permute-done.13 = bf16[2,48,768]{2,1,0:T(8,128)(2,1)S(1)} collective-permute-done((bf16[2,48,768]{2,1,0:T(8,128)(2,1)S(1)}, bf16[2,48,768]{2,1,0:T(8,128)(2,1)S(1)}, u32[]{:S(2)}, u32[]{:S(2)}) %collective-permute-start.13) | collective-permute-done | bytes 147488 | tf_op jit(solution)/shard_map/ppermute | solution.py:465
  234.3 3.2 %collective-permute-start.14 = (bf16[48,768]{1,0:T(8,128)(2,1)S(1)}, bf16[48,768]{1,0:T(8,128)(2,1)S(1)}, u32[]{:S(2)}, u32[]{:S(2)}) collective-permute-start(bf16[48,768]{1,0:T(8,128)(2,1)S(1)} %fusion.21), channel_id=1, source_target_pairs={{0,8},{1,9},{2,10},{3,11},{4,12},{5,13},{6,14},{7,15},{8,0},{9,1},... | collective-permute-start | bytes 221192 | tf_op jit(solution)/shard_map/ppermute | solution.py:465
  238.7 1.5 collective-permute-start.9
  240.3 4.4 %collective-permute-done.20 = bf16[2,2,192,768]{3,2,1,0:T(8,128)(2,1)S(1)} collective-permute-done((bf16[2,2,192,768]{3,2,1,0:T(8,128)(2,1)S(1)}, bf16[2,2,192,768]{3,2,1,0:T(8,128)(2,1)S(1)}, u32[]{:S(2)}, u32[]{:S(2)}) %collective-permute-start.20) | collective-permute-done | bytes 1179680 | tf_op jit(solution)/shard_map/ppermute | solution.py:465
  244.7 1.3 fusion.2
  246.9 23.0 %collective-permute-done.16 = bf16[2,2,48,3072]{3,2,1,0:T(8,128)(2,1)S(1)} collective-permute-done((bf16[2,2,48,3072]{3,2,1,0:T(8,128)(2,1)S(1)}, bf16[2,2,48,3072]{3,2,1,0:T(8,128)(2,1)S(1)}, u32[]{:S(2)}, u32[]{:S(2)}) %collective-permute-start.16) | collective-permute-done | bytes 1179680 | tf_op jit(solution)/shard_map/ppermute | solution.py:465
  269.9 1.3 fusion.3
  272.9 2.6 collective-permute-done.9
  276.6 3.1 collective-permute-start.10
  280.8 4.3 %collective-permute-done.17 = bf16[2,48,3072]{2,1,0:T(8,128)(2,1)S(1)} collective-permute-done((bf16[2,48,3072]{2,1,0:T(8,128)(2,1)S(1)}, bf16[2,48,3072]{2,1,0:T(8,128)(2,1)S(1)}, u32[]{:S(2)}, u32[]{:S(2)}) %collective-permute-start.17) | collective-permute-done | bytes 589856 | tf_op jit(solution)/shard_map/ppermute | solution.py:465
  286.2 5.4 %collective-permute-start.18 = (bf16[48,3072]{1,0:T(8,128)(2,1)S(1)}, bf16[48,3072]{1,0:T(8,128)(2,1)S(1)}, u32[]{:S(2)}, u32[]{:S(2)}) collective-permute-start(bf16[48,3072]{1,0:T(8,128)(2,1)S(1)} %fusion.9), channel_id=1, source_target_pairs={{0,8},{1,9},{2,10},{3,11},{4,12},{5,13},{6,14},{7,15},{8,0},{9,1},... | collective-permute-start | bytes 884744 | tf_op jit(solution)/shard_map/ppermute | solution.py:465
  291.6 9.2 %collective-permute-done.10 = bf16[48,2304]{1,0:T(8,128)(2,1)S(1)} collective-permute-done((bf16[48,2304]{1,0:T(8,128)(2,1)S(1)}, bf16[48,2304]{1,0:T(8,128)(2,1)S(1)}, u32[]{:S(2)}, u32[]{:S(2)}) %collective-permute-start.10) | collective-permute-done | bytes 221216 | tf_op jit(solution)/shard_map/ppermute | solution.py:465
  300.8 1.8 fusion.15
  302.6 4.5 %collective-permute-done.22 = bf16[192,768]{1,0:T(8,128)(2,1)S(1)} collective-permute-done((bf16[192,768]{1,0:T(8,128)(2,1)S(1)}, bf16[192,768]{1,0:T(8,128)(2,1)S(1)}, u32[]{:S(2)}, u32[]{:S(2)}) %collective-permute-start.22) | collective-permute-done | bytes 294944 | tf_op jit(solution)/shard_map/ppermute | solution.py:465
  307.1 2.0 fusion.8
  309.2 2.3 collective-permute-done.18
  311.4 2.0 fusion.11
  (134 shorter events, 36.3 us)
Async XLA Ops:
  0.6 2.9 copy-start
  26.7 10.9 %collective-permute-start = (bf16[256,768]{1,0:T(8,128)(2,1)}, bf16[256,768]{1,0:T(8,128)(2,1)S(1)}, u32[]{:S(2)}, u32[]{:S(2)}) collective-permute-start(bf16[256,768]{1,0:T(8,128)(2,1)} %relay_forward.1), channel_id=1, source_target_pairs={{0,16},{1,17},{2,18},{3,19},{4,20},{5,21},{6,22},{7,23},{8,24},{9,... | collective-permute-start | bytes 1179656 | tf_op jit(solution)/shard_map/ppermute | solution.py:523
  56.1 25.1 %collective-permute-start.1 = (bf16[256,768]{1,0:T(8,128)(2,1)}, bf16[256,768]{1,0:T(8,128)(2,1)S(1)}, u32[]{:S(2)}, u32[]{:S(2)}) collective-permute-start(bf16[256,768]{1,0:T(8,128)(2,1)} %get-tuple-element.50), channel_id=1, source_target_pairs={{0,16},{16,0},{1,17},{17,1},{2,18},{18,2},{3,19},{19,3},{4,20},{20... | collective-permute-start | bytes 1179656 | tf_op jit(solution)/shard_map/ppermute | solution.py:525
  113.2 12.5 %collective-permute-start.2 = (bf16[256,768]{1,0:T(8,128)(2,1)}, bf16[256,768]{1,0:T(8,128)(2,1)S(1)}, u32[]{:S(2)}, u32[]{:S(2)}) collective-permute-start(bf16[256,768]{1,0:T(8,128)(2,1)} %get-tuple-element.52), channel_id=1, source_target_pairs={{16,0},{17,1},{18,2},{19,3},{20,4},{21,5},{22,6},{23,7},{24,8},{25... | collective-permute-start | bytes 1179656 | tf_op jit(solution)/shard_map/ppermute | solution.py:527
  126.4 32.3 %copy-start.27 = (f32[8,3072]{1,0:T(8,128)S(1)}, f32[8,3072]{1,0:T(8,128)}, u32[]{:S(2)}) copy-start(f32[8,3072]{1,0:T(8,128)} %get-tuple-element.64) | copy-start | bytes 294916
  126.4 33.3 %copy-start.15 = (bf16[256,3072]{1,0:T(8,128)(2,1)S(1)}, bf16[256,3072]{1,0:T(8,128)(2,1)}, u32[]{:S(2)}) copy-start(bf16[256,3072]{1,0:T(8,128)(2,1)} %get-tuple-element.84.left_x) | copy-start | bytes 4718596
  126.4 33.4 %copy-start.21 = (bf16[256,768]{1,0:T(8,128)(2,1)S(1)}, bf16[256,768]{1,0:T(8,128)(2,1)}, u32[]{:S(2)}) copy-start(bf16[256,768]{1,0:T(8,128)(2,1)} %get-tuple-element.86.right_x) | copy-start | bytes 1179652
  159.7 1.4 copy-start.6
  162.1 7.8 %copy-start.7 = (bf16[256,3072]{1,0:T(8,128)(2,1)S(1)}, bf16[256,3072]{1,0:T(8,128)(2,1)}, u32[]{:S(2)}) copy-start(bf16[256,3072]{1,0:T(8,128)(2,1)} %get-tuple-element.81.right_y) | copy-start | bytes 4718596
  162.1 7.8 %copy-start.11 = (bf16[256,768]{1,0:T(8,128)(2,1)S(1)}, bf16[256,768]{1,0:T(8,128)(2,1)}, u32[]{:S(2)}) copy-start(bf16[256,768]{1,0:T(8,128)(2,1)} %get-tuple-element.79.left_y) | copy-start | bytes 1179652
  162.1 7.8 %copy-start.14 = (bf16[256,3072]{1,0:T(8,128)(2,1)S(1)}, bf16[256,3072]{1,0:T(8,128)(2,1)}, u32[]{:S(2)}) copy-start(bf16[256,3072]{1,0:T(8,128)(2,1)} %get-tuple-element.80.right_x) | copy-start | bytes 4718596
  162.1 7.9 %copy-start.20 = (bf16[256,768]{1,0:T(8,128)(2,1)S(1)}, bf16[256,768]{1,0:T(8,128)(2,1)}, u32[]{:S(2)}) copy-start(bf16[256,768]{1,0:T(8,128)(2,1)} %get-tuple-element.78.left_x) | copy-start | bytes 1179652
  167.8 2.2 copy-start.2
  170.0 43.3 %collective-permute-start.19 = (bf16[8,192,768]{2,1,0:T(8,128)(2,1)}, bf16[8,192,768]{2,1,0:T(8,128)(2,1)}, u32[]{:S(2)}, u32[]{:S(2)}) collective-permute-start(bf16[8,192,768]{2,1,0:T(8,128)(2,1)} %get-tuple-element.89), channel_id=1, source_target_pairs={{0,1},{1,0},{2,3},{3,2},{4,5},{5,4},{6,7},{7,6},{8,9},{9,8},{10,11... | collective-permute-start | bytes 7077896 | tf_op jit(solution)/shard_map/ppermute | solution.py:465
  176.1 2.2 copy-start.3
  178.2 39.1 %collective-permute-start.15 = (bf16[8,48,3072]{2,1,0:T(8,128)(2,1)}, bf16[8,48,3072]{2,1,0:T(8,128)(2,1)}, u32[]{:S(2)}, u32[]{:S(2)}) collective-permute-start(bf16[8,48,3072]{2,1,0:T(8,128)(2,1)} %get-tuple-element.83), channel_id=1, source_target_pairs={{0,1},{1,0},{2,3},{3,2},{4,5},{5,4},{6,7},{7,6},{8,9},{9,8},{10,11... | collective-permute-start | bytes 7077896 | tf_op jit(solution)/shard_map/ppermute | solution.py:465
  180.3 1.7 copy-start.16
  180.3 1.8 copy-start.19
  180.4 8.4 %collective-permute-start.3 = (bf16[8,8,2816]{2,1,0:T(8,128)(2,1)S(1)}, bf16[8,8,2816]{2,1,0:T(8,128)(2,1)S(1)}, u32[]{:S(2)}, u32[]{:S(2)}) collective-permute-start(bf16[8,8,2816]{2,1,0:T(8,128)(2,1)S(1)} %fusion.16), channel_id=1, source_target_pairs={{0,1},{1,0},{2,3},{3,2},{4,5},{5,4},{6,7},{7,6},{8,9},{9,8},{10,11... | collective-permute-start | bytes 1081352 | tf_op jit(solution)/shard_map/ppermute | solution.py:465
  186.7 1.9 copy-start.4
  188.6 2.9 copy-start.10
  188.6 2.9 copy-start.13
  188.6 2.9 copy-start.17
  188.6 2.9 copy-start.18
  188.6 21.6 %collective-permute-start.7 = (bf16[8,48,2304]{2,1,0:T(8,128)(2,1)}, bf16[8,48,2304]{2,1,0:T(8,128)(2,1)}, u32[]{:S(2)}, u32[]{:S(2)}) collective-permute-start(bf16[8,48,2304]{2,1,0:T(8,128)(2,1)} %get-tuple-element.71), channel_id=1, source_target_pairs={{0,1},{1,0},{2,3},{3,2},{4,5},{5,4},{6,7},{7,6},{8,9},{9,8},{10,11... | collective-permute-start | bytes 5308424 | tf_op jit(solution)/shard_map/ppermute | solution.py:465
  188.8 1.6 copy-start.26
  190.4 7.3 %collective-permute-start.4 = (bf16[2,2,8,2816]{3,2,1,0:T(8,128)(2,1)}, bf16[2,2,8,2816]{3,2,1,0:T(8,128)(2,1)}, u32[]{:S(2)}, u32[]{:S(2)}) collective-permute-start(bf16[2,2,8,2816]{3,2,1,0:T(8,128)(2,1)} %fusion.19), channel_id=1, source_target_pairs={{0,2},{1,3},{2,0},{3,1},{4,6},{5,7},{6,4},{7,5},{8,10},{9,11},{10,... | collective-permute-start | bytes 540680 | tf_op jit(solution)/shard_map/ppermute | solution.py:465
  192.7 13.8 %collective-permute-start.11 = (bf16[8,48,768]{2,1,0:T(8,128)(2,1)S(1)}, bf16[8,48,768]{2,1,0:T(8,128)(2,1)S(1)}, u32[]{:S(2)}, u32[]{:S(2)}) collective-permute-start(bf16[8,48,768]{2,1,0:T(8,128)(2,1)S(1)} %get-tuple-element.77), channel_id=1, source_target_pairs={{0,1},{1,0},{2,3},{3,2},{4,5},{5,4},{6,7},{7,6},{8,9},{9,8},{10,11... | collective-permute-start | bytes 1769480 | tf_op jit(solution)/shard_map/ppermute | solution.py:465
  198.7 4.6 %collective-permute-start.5 = (bf16[2,8,2816]{2,1,0:T(8,128)(2,1)S(1)}, bf16[2,8,2816]{2,1,0:T(8,128)(2,1)S(1)}, u32[]{:S(2)}, u32[]{:S(2)}) collective-permute-start(bf16[2,8,2816]{2,1,0:T(8,128)(2,1)S(1)} %fusion.20), channel_id=1, source_target_pairs={{0,4},{1,5},{2,6},{3,7},{4,0},{5,1},{6,2},{7,3},{8,12},{9,13},{10,... | collective-permute-start | bytes 270344 | tf_op jit(solution)/shard_map/ppermute | solution.py:465
  204.2 5.0 %collective-permute-start.6 = (bf16[8,2816]{1,0:T(8,128)(2,1)S(1)}, bf16[8,2816]{1,0:T(8,128)(2,1)S(1)}, u32[]{:S(2)}, u32[]{:S(2)}) collective-permute-start(bf16[8,2816]{1,0:T(8,128)(2,1)S(1)} %fusion.26), channel_id=1, source_target_pairs={{0,8},{1,9},{2,10},{3,11},{4,12},{5,13},{6,14},{7,15},{8,0},{9,1},... | collective-permute-start | bytes 135176 | tf_op jit(solution)/shard_map/ppermute | solution.py:465
  206.5 10.9 %slice-start.2 = ((s8[4718592]{0:T(1024)(128)(4,1)}), s8[4194304]{0:T(1024)(128)(4,1)S(1)}, s32[]{:S(2)}) async-start(s8[4718592]{0:T(1024)(128)(4,1)} %bitcast.189), calls=%async_computation.2 | async-start | bytes 8388608
  206.5 15.0 %collective-permute-start.12 = (bf16[2,2,48,768]{3,2,1,0:T(8,128)(2,1)S(1)}, bf16[2,2,48,768]{3,2,1,0:T(8,128)(2,1)S(1)}, u32[]{:S(2)}, u32[]{:S(2)}) collective-permute-start(bf16[2,2,48,768]{3,2,1,0:T(8,128)(2,1)S(1)} %fusion.17), channel_id=1, source_target_pairs={{0,2},{1,3},{2,0},{3,1},{4,6},{5,7},{6,4},{7,5},{8,10},{9,11},{10,... | collective-permute-start | bytes 884744 | tf_op jit(solution)/shard_map/ppermute | solution.py:465
  210.2 7.2 %slice-start.3 = ((s8[4718592]{0:T(1024)(128)(4,1)}), s8[524288]{0:T(1024)(128)(4,1)S(1)}, s32[]{:S(2)}) async-start(s8[4718592]{0:T(1024)(128)(4,1)} %bitcast.189), calls=%async_computation.3 | async-start | bytes 1048576
  212.1 25.4 %collective-permute-start.8 = (bf16[2,2,48,2304]{3,2,1,0:T(8,128)(2,1)S(1)}, bf16[2,2,48,2304]{3,2,1,0:T(8,128)(2,1)S(1)}, u32[]{:S(2)}, u32[]{:S(2)}) collective-permute-start(bf16[2,2,48,2304]{3,2,1,0:T(8,128)(2,1)S(1)} %fusion.4), channel_id=1, source_target_pairs={{0,4},{1,5},{2,6},{3,7},{4,0},{5,1},{6,2},{7,3},{8,12},{9,13},{10,... | collective-permute-start | bytes 2654216 | tf_op jit(solution)/shard_map/ppermute | solution.py:465
  213.3 31.4 %slice-start = ((s8[4718592]{0:T(1024)(128)(4,1)}), s8[4194304]{0:T(1024)(128)(4,1)S(1)}, s32[]{:S(2)}) async-start(s8[4718592]{0:T(1024)(128)(4,1)} %bitcast.184), calls=%async_computation | async-start | bytes 8388608
  215.7 29.0 %collective-permute-start.20 = (bf16[2,2,192,768]{3,2,1,0:T(8,128)(2,1)S(1)}, bf16[2,2,192,768]{3,2,1,0:T(8,128)(2,1)S(1)}, u32[]{:S(2)}, u32[]{:S(2)}) collective-permute-start(bf16[2,2,192,768]{3,2,1,0:T(8,128)(2,1)S(1)} %fusion.1), channel_id=1, source_target_pairs={{0,2},{1,3},{2,0},{3,1},{4,6},{5,7},{6,4},{7,5},{8,10},{9,11},{10,... | collective-permute-start | bytes 3538952 | tf_op jit(solution)/shard_map/ppermute | solution.py:465
  217.4 20.2 %copy-start.5 = (f32[8,48,2304]{2,1,0:T(8,128)S(1)}, f32[8,48,2304]{2,1,0:T(8,128)}, u32[]{:S(2)}) copy-start(f32[8,48,2304]{2,1,0:T(8,128)} %copy-done.4) | copy-start | bytes 10616836
  217.4 27.3 %slice-start.1 = ((s8[4718592]{0:T(1024)(128)(4,1)}), s8[524288]{0:T(1024)(128)(4,1)S(1)}, s32[]{:S(2)}) async-start(s8[4718592]{0:T(1024)(128)(4,1)} %bitcast.184), calls=%async_computation.1 | async-start | bytes 1048576
  219.2 50.8 %collective-permute-start.16 = (bf16[2,2,48,3072]{3,2,1,0:T(8,128)(2,1)S(1)}, bf16[2,2,48,3072]{3,2,1,0:T(8,128)(2,1)S(1)}, u32[]{:S(2)}, u32[]{:S(2)}) collective-permute-start(bf16[2,2,48,3072]{3,2,1,0:T(8,128)(2,1)S(1)} %fusion), channel_id=1, source_target_pairs={{0,2},{1,3},{2,0},{3,1},{4,6},{5,7},{6,4},{7,5},{8,10},{9,11},{10,... | collective-permute-start | bytes 3538952 | tf_op jit(solution)/shard_map/ppermute | solution.py:465
  221.6 12.7 %collective-permute-start.13 = (bf16[2,48,768]{2,1,0:T(8,128)(2,1)S(1)}, bf16[2,48,768]{2,1,0:T(8,128)(2,1)S(1)}, u32[]{:S(2)}, u32[]{:S(2)}) collective-permute-start(bf16[2,48,768]{2,1,0:T(8,128)(2,1)S(1)} %fusion.18), channel_id=1, source_target_pairs={{0,4},{1,5},{2,6},{3,7},{4,0},{5,1},{6,2},{7,3},{8,12},{9,13},{10,... | collective-permute-start | bytes 442376 | tf_op jit(solution)/shard_map/ppermute | solution.py:465
  234.3 37.9 %collective-permute-start.14 = (bf16[48,768]{1,0:T(8,128)(2,1)S(1)}, bf16[48,768]{1,0:T(8,128)(2,1)S(1)}, u32[]{:S(2)}, u32[]{:S(2)}) collective-permute-start(bf16[48,768]{1,0:T(8,128)(2,1)S(1)} %fusion.21), channel_id=1, source_target_pairs={{0,8},{1,9},{2,10},{3,11},{4,12},{5,13},{6,14},{7,15},{8,0},{9,1},... | collective-permute-start | bytes 221192 | tf_op jit(solution)/shard_map/ppermute | solution.py:465
  238.7 36.8 %collective-permute-start.9 = (bf16[2,48,2304]{2,1,0:T(8,128)(2,1)S(1)}, bf16[2,48,2304]{2,1,0:T(8,128)(2,1)S(1)}, u32[]{:S(2)}, u32[]{:S(2)}) collective-permute-start(bf16[2,48,2304]{2,1,0:T(8,128)(2,1)S(1)} %fusion.5), channel_id=1, source_target_pairs={{0,2},{1,3},{2,0},{3,1},{4,6},{5,7},{6,4},{7,5},{8,10},{9,11},{10,... | collective-permute-start | bytes 1327112 | tf_op jit(solution)/shard_map/ppermute | solution.py:465
  246.0 33.7 %collective-permute-start.21 = (bf16[2,192,768]{2,1,0:T(8,128)(2,1)S(1)}, bf16[2,192,768]{2,1,0:T(8,128)(2,1)S(1)}, u32[]{:S(2)}, u32[]{:S(2)}) collective-permute-start(bf16[2,192,768]{2,1,0:T(8,128)(2,1)S(1)} %fusion.2), channel_id=1, source_target_pairs={{0,4},{1,5},{2,6},{3,7},{4,0},{5,1},{6,2},{7,3},{8,12},{9,13},{10,... | collective-permute-start | bytes 1769480 | tf_op jit(solution)/shard_map/ppermute | solution.py:465
  271.2 13.9 %collective-permute-start.17 = (bf16[2,48,3072]{2,1,0:T(8,128)(2,1)S(1)}, bf16[2,48,3072]{2,1,0:T(8,128)(2,1)S(1)}, u32[]{:S(2)}, u32[]{:S(2)}) collective-permute-start(bf16[2,48,3072]{2,1,0:T(8,128)(2,1)S(1)} %fusion.3), channel_id=1, source_target_pairs={{0,4},{1,5},{2,6},{3,7},{4,0},{5,1},{6,2},{7,3},{8,12},{9,13},{10,... | collective-permute-start | bytes 1769480 | tf_op jit(solution)/shard_map/ppermute | solution.py:465
  276.6 24.2 %collective-permute-start.10 = (bf16[48,2304]{1,0:T(8,128)(2,1)S(1)}, bf16[48,2304]{1,0:T(8,128)(2,1)S(1)}, u32[]{:S(2)}, u32[]{:S(2)}) collective-permute-start(bf16[48,2304]{1,0:T(8,128)(2,1)S(1)} %fusion.13), channel_id=1, source_target_pairs={{0,8},{1,9},{2,10},{3,11},{4,12},{5,13},{6,14},{7,15},{8,0},{9,1},... | collective-permute-start | bytes 663560 | tf_op jit(solution)/shard_map/ppermute | solution.py:465
  280.7 26.4 %collective-permute-start.22 = (bf16[192,768]{1,0:T(8,128)(2,1)S(1)}, bf16[192,768]{1,0:T(8,128)(2,1)S(1)}, u32[]{:S(2)}, u32[]{:S(2)}) collective-permute-start(bf16[192,768]{1,0:T(8,128)(2,1)S(1)} %fusion.6), channel_id=1, source_target_pairs={{0,8},{1,9},{2,10},{3,11},{4,12},{5,13},{6,14},{7,15},{8,0},{9,1},... | collective-permute-start | bytes 884744 | tf_op jit(solution)/shard_map/ppermute | solution.py:465
  286.2 25.2 %collective-permute-start.18 = (bf16[48,3072]{1,0:T(8,128)(2,1)S(1)}, bf16[48,3072]{1,0:T(8,128)(2,1)S(1)}, u32[]{:S(2)}, u32[]{:S(2)}) collective-permute-start(bf16[48,3072]{1,0:T(8,128)(2,1)S(1)} %fusion.9), channel_id=1, source_target_pairs={{0,8},{1,9},{2,10},{3,11},{4,12},{5,13},{6,14},{7,15},{8,0},{9,1},... | collective-permute-start | bytes 884744 | tf_op jit(solution)/shard_map/ppermute | solution.py:465
  307.1 6.3 %copy-start.1 = (bf16[1,128,2304]{2,1,0:T(8,128)(2,1)S(1)}, bf16[1,128,2304]{2,1,0:T(8,128)(2,1)}, u32[]{:S(2)}) copy-start(bf16[1,128,2304]{2,1,0:T(8,128)(2,1)} %param.18) | copy-start | bytes 1769476
  (7 other events, 6.7 us)
